TPU v7x, 256 devices: a whole 4x4x8 slice. The times are simulated.
256 devices in a mesh: ctx: 8 (over x_lo, y), req: 32 (over x_hi, z, core).
Axes of the slice: x: 4 (x_hi: 2, x_lo: 2; x = x_hi * 2 + x_lo), y: 4, z: 8, core: 2. Of those that a mesh axis runs over, the one named last changes fastest.
Arguments:
- queries: bfloat16 [16384, 1024], P(('ctx', 'req')), may hold values from -12 to 12
- suffix_keys: bfloat16 [16384, 128], P(('ctx', 'req')), may hold values from -10 to 10
- suffix_values: bfloat16 [16384, 128], P(('ctx', 'req')), may hold values from -6 to 6
- prefix_keys: bfloat16 [32768, 128], P(('ctx', 'req')), may hold values from -7.5 to 7.5
- prefix_values: bfloat16 [32768, 128], P(('ctx', 'req')), may hold values from -6 to 6
- slot_request: int32 [16384], P(('ctx', 'req')), may hold values from 0 to 64, as said below
Outputs:
- attended: bfloat16 [16384, 1024], P(('ctx', 'req'))
Inputs may be any that keep to these rules, and one draw needn't show every extreme that they name: `slot_request`: on each device the live slots come first and hold requests numbered 0, 1, 2 and so on in order, the slots of a request consecutive; empty slots hold 64. The devices with one index of ctx hold 32 times their number of live slots together, and one of them has all 64 slots live. Numbering the live slots of the devices with one index of ctx in order of req index and then slot, and giving each to the req index equal to its number modulo the number of devices along req, every device is given exactly 32 slots.
All inputs are finite; a program needn't handle non-finite values.
Results may differ from a plain program's by a relative error of at most 0.017.
Values may be sent and summed in bfloat16 or wider, within the bound.
No kernel may reach another device: no remote copies, remote signals or barrier semaphores. Data moves between devices by JAX's collectives and lax.ppermute only.
A program may use at most 64 MiB of HBM per device.

v0:
```python
import math

import jax
import jax.numpy as jnp
from jax import lax
from jax.sharding import PartitionSpec as P

H = 8
HD = 128


MASKED_SCORE = -1e30


def key_folder(query_block, state_in, key_piece):
    row_count = query_block.shape[0]
    score_scale = 1.0 / math.sqrt(HD)
    key_rows, value_rows = key_piece
    piece_length = key_rows.shape[0]
    block_size = math.gcd(piece_length, max(128, 131072 // row_count))

    def one_block(position, block_state):
        numerator, mass_total, row_peak = block_state
        key_block = lax.dynamic_slice_in_dim(key_rows, position * block_size, block_size, 0)
        value_block = lax.dynamic_slice_in_dim(value_rows, position * block_size, block_size, 0)
        scores = (
            jnp.einsum("rhd,nd->rhn", query_block, key_block, preferred_element_type=jnp.float32)
            * score_scale
        )
        new_peak = jnp.maximum(row_peak, jnp.max(scores, axis=-1))
        weights = jnp.exp(scores - new_peak[..., None])
        shrink = jnp.exp(row_peak - new_peak)
        mass_total = mass_total * shrink + jnp.sum(weights, axis=-1)
        numerator = numerator * shrink[..., None] + jnp.einsum(
            "rhn,nd->rhd",
            weights.astype(jnp.bfloat16),
            value_block,
            preferred_element_type=jnp.float32,
        )
        return (numerator, mass_total, new_peak)

    return lax.fori_loop(0, piece_length // block_size, one_block, state_in)


def empty_state(row_count):
    return (
        jnp.zeros((row_count, H, HD), jnp.float32),
        jnp.zeros((row_count, H), jnp.float32),
        jnp.full((row_count, H), MASKED_SCORE, jnp.float32),
    )


def prefix_states(query_rows, prefix_keys, prefix_values):
    row_count = query_rows.shape[0]
    query_block = query_rows.reshape(row_count, H, HD)
    return key_folder(
        query_block,
        empty_state(row_count),
        (
            lax.all_gather(prefix_keys, ("ctx", "req"), axis=0, tiled=True),
            lax.all_gather(prefix_values, ("ctx", "req"), axis=0, tiled=True),
        ),
    )


def suffix_state(queries, suffix_keys, suffix_values, slot_request):
    slot_count = queries.shape[0]
    score_scale = 1.0 / math.sqrt(HD)
    query_block = queries.reshape(slot_count, H, HD)
    scores = (
        jnp.einsum("rhd,nd->rhn", query_block, suffix_keys, preferred_element_type=jnp.float32)
        * score_scale
    )
    query_index = lax.broadcasted_iota(jnp.int32, (slot_count, slot_count), 0)
    key_index = lax.broadcasted_iota(jnp.int32, (slot_count, slot_count), 1)
    visible = (slot_request[:, None] == slot_request[None, :]) & (key_index <= query_index)
    scores = jnp.where(visible[:, None, :], scores, MASKED_SCORE)
    row_peak = jnp.max(scores, axis=-1)
    weights = jnp.exp(scores - row_peak[..., None])
    mass_total = jnp.sum(weights, axis=-1)
    numerator = jnp.einsum(
        "rhn,nd->rhd",
        weights.astype(jnp.bfloat16),
        suffix_values,
        preferred_element_type=jnp.float32,
    )
    return (numerator, mass_total, row_peak)


def combine_states(prefix_part, suffix_part, live_mask):
    prefix_sum, prefix_mass, prefix_peak = prefix_part
    suffix_sum, suffix_mass, suffix_peak = suffix_part
    row_peak = jnp.maximum(prefix_peak, suffix_peak)
    prefix_factor = jnp.exp(prefix_peak - row_peak)
    suffix_factor = jnp.exp(suffix_peak - row_peak)
    upper = prefix_sum * prefix_factor[..., None] + suffix_sum * suffix_factor[..., None]
    lower = prefix_mass * prefix_factor + suffix_mass * suffix_factor
    merged = upper / lower[..., None]
    slot_count = merged.shape[0]
    merged = merged.reshape(slot_count, -1)
    return jnp.where(live_mask[:, None], merged, 0.0).astype(jnp.bfloat16)


def per_device(queries, suffix_keys, suffix_values, prefix_keys, prefix_values, slot_request):
    slot_count = queries.shape[0]
    suffix_part = suffix_state(queries, suffix_keys, suffix_values, slot_request)
    prefix_part = prefix_states(queries, prefix_keys, prefix_values)
    return combine_states(prefix_part, suffix_part, slot_request < slot_count)


def solution(mesh):
    placed = (
        P(("ctx", "req"), None),
        P(("ctx", "req"), None),
        P(("ctx", "req"), None),
        P(("ctx", "req"), None),
        P(("ctx", "req"), None),
        P(("ctx", "req")),
    )
    return jax.shard_map(
        per_device, mesh=mesh, in_specs=placed, out_specs=P(("ctx", "req"), None), check_vma=False
    )
```

profile of v0, /device:TPU:32, one launch (start us, length us, event | category | flops | bytes accessed | tf_op | source)
XLA Modules:
  0.0 1005.9 jit_solution(2364517838533187497)
XLA Ops:
  12.8 419.4 %all-gather.3.cloned.1.call-done = bf16[32768,128]{1,0:T(8,128)(2,1)} async-done(((bf16[128,128]{1,0:T(8,128)(2,1)}), bf16[32768,128]{1,0:T(8,128)(2,1)}) %all-gather.3.cloned.1.call-update) | async-done | bytes 8388624 | tf_op jit(solution)/shard_map/all_gather | solution.py:60
  432.1 418.8 %all-gather.5.cloned.1.call-done = bf16[32768,128]{1,0:T(8,128)(2,1)} async-done(((bf16[128,128]{1,0:T(8,128)(2,1)}), bf16[32768,128]{1,0:T(8,128)(2,1)}) %all-gather.5.cloned.1.call-update) | async-done | bytes 8388624 | tf_op jit(solution)/shard_map/all_gather | solution.py:61
  850.9 146.8 %while.18 = (s32[]{:T(128)}, f32[64,8,128]{2,0,1:T(8,128)S(1)}, f32[64,8]{0,1:T(8,128)S(1)}, f32[64,8]{0,1:T(8,128)S(1)}, bf16[32768,128]{1,0:T(8,128)(2,1)}, /*...) while((s32[]{:T(128)}, f32[64,8,128]{2,0,1:T(8,128)S(1)}, ...), condition=%wide.region_3.0_spmd.clone, body=%wide.region_0.3_spmd.clone.sunk | while | flops 545458688 | bytes 31097040 | solution.py:42
  850.9 3.7 bitcast_reduce_fusion.2
  854.6 3.2 fusion.47
  860.1 3.7 bitcast_reduce_fusion.2
  863.8 3.2 fusion.47
  869.3 3.7 bitcast_reduce_fusion.2
  873.0 3.2 fusion.47
  878.4 3.7 bitcast_reduce_fusion.2
  882.1 3.2 fusion.47
  887.6 3.7 bitcast_reduce_fusion.2
  891.3 3.2 fusion.47
  896.8 3.7 bitcast_reduce_fusion.2
  900.5 3.2 fusion.47
  906.0 3.7 bitcast_reduce_fusion.2
  909.7 3.2 fusion.47
  915.1 3.7 bitcast_reduce_fusion.2
  918.8 3.2 fusion.47
  924.3 3.7 bitcast_reduce_fusion.2
  928.0 3.2 fusion.47
  933.5 3.7 bitcast_reduce_fusion.2
  937.2 3.2 fusion.47
  942.7 3.7 bitcast_reduce_fusion.2
  946.3 3.2 fusion.47
  951.8 3.7 bitcast_reduce_fusion.2
  961.0 3.7 bitcast_reduce_fusion.2
  964.7 3.2 fusion.47
  970.2 3.7 bitcast_reduce_fusion.2
  979.3 3.7 bitcast_reduce_fusion.2
  988.5 3.7 bitcast_reduce_fusion.2
  992.2 3.2 fusion.47
  (122 shorter events, 53.6 us)
Async XLA Ops:
  6.5 991.4 %copy-start = (bf16[64,128]{1,0:T(8,128)(2,1)S(1)}, bf16[64,128]{1,0:T(8,128)(2,1)}, u32[]{:S(2)}) copy-start(bf16[64,128]{1,0:T(8,128)(2,1)} %param.10) | copy-start | bytes 49156
  6.5 425.6 %all-gather.3.cloned.1.call-start = ((), (), s32[]{:S(2)}) async-start(), calls=%async_computation | async-start | bytes 8421376 | tf_op jit(solution)/shard_map/all_gather | solution.py:60
  7.3 843.7 %all-gather.5.cloned.1.call-start = ((), (), s32[]{:S(2)}) async-start(), calls=%async_computation.1 | async-start | bytes 8421376 | tf_op jit(solution)/shard_map/all_gather | solution.py:61
  854.6 3.4 copy-start.1
  863.8 3.4 copy-start.1
  873.0 3.4 copy-start.1
  882.1 3.4 copy-start.1
  891.3 3.4 copy-start.1
  900.5 3.4 copy-start.1
  909.6 3.4 copy-start.1
  918.8 3.4 copy-start.1
  928.0 3.4 copy-start.1
  937.2 3.4 copy-start.1
  946.3 3.4 copy-start.1
  955.5 3.4 copy-start.1
  964.7 3.4 copy-start.1
  973.9 3.4 copy-start.1
  983.0 3.4 copy-start.1
  992.2 3.4 copy-start.1
Sparse Core Ops, SparseCore 0:
  9.2 422.8 all-gather.2
  434.0 416.8 all-gather.4
where the time goes:
time: 1010 us
  waiting for transfers between devices  840 us (83%)
  matrix products  92.4 us (9%)
  other arithmetic  53.4 us (5%)
  between operations  13.5 us (1%)
    all_gather x1, waiting for transfers between devices, prefix_states(): lax.all_gather(prefix_keys, ('ctx', 'req'), axis=0, tiled=True)  419 us
    all_gather x1, waiting for transfers between devices, prefix_states(): lax.all_gather(prefix_values, ('ctx', 'req'), axis=0, tiled=True)  419 us
    dot_general x16, matrix products, one_block(): jnp.einsum('rhd,nd->rhn', query_block, key_block, preferred_element_type=...  58.9 us
    reduce_sum x16, other arithmetic, one_block(): mass_total = mass_total * shrink + jnp.sum(weights, axis=-1)  50.6 us
    dot_general x16, matrix products, one_block(): jnp.einsum('rhn,nd->rhd', weights.astype(jnp.bfloat16), value_block, pref...  32.1 us
  transfers between devices with their start and end apart: 2, of which 2 were waited for; matrix products, arithmetic and copies ran while one was open for 0% of the time, Pallas kernels for 0%

commit v1 on v0

v1 whole, which is shorter than its diff:
```python
import math

import jax
import jax.numpy as jnp
from jax import lax
from jax.experimental import pallas as pl
from jax.experimental.pallas import tpu as pltpu
from jax.sharding import PartitionSpec as P

H = 8
HD = 128
AXES = ("ctx", "req")
SCALE = 1.4426950408889634 / math.sqrt(HD)
MASKED_SCORE = -1e30
BLOCK = 128
POOL = 4
KEY_TILE = 512
ROW_TILE = 256
TILES_AT_ONCE = 4

f32, bf16 = jnp.float32, jnp.bfloat16
VMEM = pl.BlockSpec(memory_space=pltpu.VMEM)
PARAMS = pltpu.CompilerParams(vmem_limit_bytes=56 * 2**20)


def moved(array, place):
    pairs = []
    for x in range(4):
        for y in range(4):
            for z in range(8):
                for c in range(2):
                    pairs.append((linear(x, y, z, c), linear(*place(x, y, z, c))))
    return lax.ppermute(array, AXES, sorted(pairs))


def linear(x, y, z, c):
    return ((x % 2) * 4 + y) * 32 + (x // 2) * 16 + z * 2 + c


def by_xor(array, dx=0, dy=0, dz=0, dc=0):
    return moved(array, lambda x, y, z, c: (x ^ dx, y ^ dy, z ^ dz, c ^ dc))


def by_ring(array, dy=0, dz=0):
    return moved(array, lambda x, y, z, c: (x, (y + dy) % 4, (z + dz) % 8, c))


def wide(column_like, width):
    return jnp.concatenate([column_like] * (width // 128), axis=1)


def spread(column, rows):
    return jnp.broadcast_to(column, (rows, 128))


def queries_kernel(*refs):
    out = refs[-1]
    slots = refs[0].shape[0]
    for j, ref in enumerate(refs[:-1]):
        for h in range(H):
            scaled = ref[:, h * HD : (h + 1) * HD].astype(f32) * SCALE
            high = scaled.astype(bf16)
            low = (scaled - high.astype(f32)).astype(bf16)
            rows = pl.ds((j * H + h) * slots, slots)
            out[rows, 0:HD] = high
            out[rows, HD : 2 * HD] = low


def prepared_queries(pool):
    slots = pool[0].shape[0]
    return pl.pallas_call(
        queries_kernel,
        out_shape=jax.ShapeDtypeStruct((len(pool) * H * slots, 2 * HD), bf16),
        in_specs=[VMEM] * len(pool),
        out_specs=VMEM,
        compiler_params=PARAMS,
    )(*pool)


def load_pieces(pieces, keys, values):
    at = 0
    ones = jnp.ones((BLOCK, HD), bf16)
    for piece in pieces:
        for b in range(piece.shape[0]):
            rows = pl.ds(at, BLOCK)
            key_rows = piece[b, 0:BLOCK, :]
            keys[rows, 0:HD] = key_rows
            keys[rows, HD : 2 * HD] = key_rows
            values[rows, 0:HD] = piece[b, BLOCK : 2 * BLOCK, :]
            values[rows, HD : 2 * HD] = ones
            at += BLOCK
    return at


def fold_tiles(query, keys, values, key_count, total_in, peak_in, total, peak, first):
    row_count = query.shape[0]
    at_once = min(TILES_AT_ONCE, row_count // ROW_TILE)

    def step(i, _):
        for start in range(0, key_count, KEY_TILE):
            length = min(KEY_TILE, key_count - start)
            for u in range(at_once):
                rows = pl.ds(pl.multiple_of((i * at_once + u) * ROW_TILE, ROW_TILE), ROW_TILE)
                scores = lax.dot_general(
                    query[rows, :],
                    keys[pl.ds(start, length), :],
                    (((1,), (1,)), ((), ())),
                    preferred_element_type=f32,
                )
                block_peak = spread(jnp.max(scores, axis=1, keepdims=True), ROW_TILE)
                fresh = first and start == 0
                if fresh:
                    new_peak = block_peak
                else:
                    held_peak, held_total = (peak_in, total_in) if start == 0 else (peak, total)
                    old_peak = held_peak[rows, :]
                    new_peak = jnp.maximum(old_peak, block_peak)
                weights = jnp.exp2(scores - wide(new_peak, length)).astype(bf16)
                added = jnp.dot(weights, values[pl.ds(start, length), :], preferred_element_type=f32)
                if not fresh:
                    added = added + held_total[rows, :] * wide(jnp.exp2(old_peak - new_peak), 2 * HD)
                total[rows, :] = added
                peak[rows, :] = new_peak
        return 0

    lax.fori_loop(0, row_count // (ROW_TILE * at_once), step, 0)


def fold_kernel(piece_count, first, *refs):
    query, pieces = refs[0], refs[1 : 1 + piece_count]
    rest = refs[1 + piece_count :]
    if first:
        total, peak, keys, values = rest
        total_in = peak_in = None
    else:
        total_in, peak_in, total, peak, keys, values = rest
    key_count = load_pieces(pieces, keys, values)
    fold_tiles(query, keys, values, key_count, total_in, peak_in, total, peak, first)


def folded(query, pieces, state=None):
    first = state is None
    state = () if first else tuple(state)
    row_count = query.shape[0]
    key_count = sum(p.shape[0] for p in pieces) * BLOCK
    at = 1 + len(pieces)
    return pl.pallas_call(
        lambda *refs: fold_kernel(len(pieces), first, *refs),
        out_shape=(
            jax.ShapeDtypeStruct((row_count, 2 * HD), f32),
            jax.ShapeDtypeStruct((row_count, HD), f32),
        ),
        in_specs=[VMEM] * (at + len(state)),
        out_specs=(VMEM, VMEM),
        scratch_shapes=[pltpu.VMEM((key_count, 2 * HD), bf16)] * 2,
        input_output_aliases={} if first else {at: 0, at + 1: 1},
        compiler_params=PARAMS,
    )(query, *pieces, *state)


def message_kernel(total, peak, *outs):
    slots = outs[0].shape[0]
    lane = lax.broadcasted_iota(jnp.int32, (slots, 128), 1)
    for j, out in enumerate(outs):
        packed = jnp.zeros((slots, 128), f32)
        for h in range(H):
            rows = pl.ds((j * H + h) * slots, slots)
            mass = total[rows, HD : 2 * HD]
            out[:, h * HD : (h + 1) * HD] = (total[rows, 0:HD] / mass).astype(bf16)
            level = peak[rows, :] + jnp.log2(mass)
            one = level.astype(bf16).astype(f32)
            two = (level - one).astype(bf16).astype(f32)
            three = level - one - two
            term = jnp.where(lane % 16 == 0, one, jnp.where(lane % 16 == 1, two, three))
            packed = jnp.where((lane // 16 == h) & (lane % 16 < 3), term, packed)
        out[:, H * HD :] = packed.astype(bf16)


def messages(state, slots):
    total, peak = state
    count = total.shape[0] // (H * slots)
    return pl.pallas_call(
        message_kernel,
        out_shape=tuple(jax.ShapeDtypeStruct((slots, H * HD + 128), bf16) for _ in range(count)),
        in_specs=[VMEM, VMEM],
        out_specs=tuple([VMEM] * count),
        compiler_params=PARAMS,
    )(total, peak)


def request_column(request_row, slots):
    row = lax.broadcasted_iota(jnp.int32, (slots, slots), 0)
    column = lax.broadcasted_iota(jnp.int32, (slots, slots), 1)
    across = jnp.broadcast_to(request_row, (slots, slots))
    return jnp.sum(jnp.where(row == column, across, 0), axis=1, keepdims=True), across, row, column


def suffix_kernel(queries, key_rows, value_rows, request, quotient, level):
    slots = queries.shape[0]
    own, across, row, column = request_column(request[...], slots)
    visible = (own == across) & (column <= row)
    for h in range(H):
        scores = lax.dot_general(
            queries[:, h * HD : (h + 1) * HD],
            key_rows[...],
            (((1,), (1,)), ((), ())),
            preferred_element_type=f32,
        )
        scores = jnp.where(visible, scores * SCALE, MASKED_SCORE)
        peak = jnp.max(scores, axis=1, keepdims=True)
        weights = jnp.exp2(scores - peak)
        mass = jnp.sum(weights, axis=1, keepdims=True)
        total = jnp.dot(weights.astype(bf16), value_rows[...], preferred_element_type=f32)
        rows = pl.ds(h * slots, slots)
        quotient[rows, :] = total / mass
        level[rows, :] = spread(peak + jnp.log2(mass), slots)


def suffix_part(queries, suffix_keys, suffix_values, request_row):
    shape = jax.ShapeDtypeStruct((H * queries.shape[0], HD), f32)
    return pl.pallas_call(
        suffix_kernel,
        out_shape=(shape, shape),
        in_specs=[VMEM] * 4,
        out_specs=(VMEM, VMEM),
        compiler_params=PARAMS,
    )(queries, suffix_keys, suffix_values, request_row)


def combine_kernel(*refs):
    parts, suffix_quotient, suffix_level, request, out = refs[:-4], *refs[-4:]
    slots = out.shape[0]
    own = request_column(request[...], slots)[0]
    live = jnp.broadcast_to(own < slots, (slots, HD))
    lane = lax.broadcasted_iota(jnp.int32, (128, H * HD), 0)
    column = lax.broadcasted_iota(jnp.int32, (128, H * HD), 1)
    gather = ((lane // 16 == column // HD) & (lane % 16 < 3)).astype(bf16)
    levels = [
        jnp.dot(part[:, H * HD :], gather, preferred_element_type=f32) for part in parts
    ]
    for h in range(H):
        columns = slice(h * HD, (h + 1) * HD)
        rows = pl.ds(h * slots, slots)
        all_levels = [level[:, columns] for level in levels] + [suffix_level[rows, :]]
        all_quotients = [part[:, columns].astype(f32) for part in parts]
        all_quotients.append(suffix_quotient[rows, :])
        top = all_levels[0]
        for level in all_levels[1:]:
            top = jnp.maximum(top, level)
        upper = lower = 0.0
        for level, quotient in zip(all_levels, all_quotients):
            weight = jnp.exp2(level - top)
            upper = upper + weight * quotient
            lower = lower + weight
        out[:, columns] = jnp.where(live, upper / lower, 0.0).astype(bf16)


def combined(parts, suffix, request_row):
    slots = parts[0].shape[0]
    return pl.pallas_call(
        combine_kernel,
        out_shape=jax.ShapeDtypeStruct((slots, H * HD), bf16),
        in_specs=[VMEM] * (len(parts) + 3),
        out_specs=VMEM,
        compiler_params=PARAMS,
    )(*parts, *suffix, request_row)


def per_device(queries, suffix_keys, suffix_values, prefix_keys, prefix_values, slot_request):
    slots = queries.shape[0]
    request_row = slot_request.reshape(1, slots)
    own = jnp.concatenate([prefix_keys, prefix_values], axis=0)[None]

    far = [by_xor(own, dz=4), by_ring(own, dz=2), by_ring(own, dz=-2)]
    pool = [
        queries,
        by_xor(queries, dx=1),
        by_xor(queries, dz=1),
        by_xor(queries, dx=1, dz=1),
    ]
    first = jnp.concatenate([own, *far], axis=0)
    suffix = suffix_part(queries, suffix_keys, suffix_values, request_row)
    query = prepared_queries(pool)

    half_a, half_b = first[:2], first[2:]
    a_x = by_xor(half_a, dx=2)
    b_y = [by_ring(half_b, dy=1), by_ring(half_b, dy=-1), by_xor(half_b, dy=2)]
    first_c = by_xor(first, dc=1)
    state = folded(query, [first])

    second_a = jnp.concatenate([half_a, a_x], axis=0)
    second_b = jnp.concatenate([half_b, *b_y], axis=0)
    a_y = [by_ring(second_a, dy=1), by_ring(second_a, dy=-1), by_xor(second_a, dy=2)]
    b_x = by_xor(second_b, dx=2)
    second = [a_x, *b_y]
    second_c = by_xor(jnp.concatenate(second, axis=0), dc=1)
    state = folded(query, [first_c, *second], state)

    third_c = by_xor(jnp.concatenate(a_y[:2], axis=0), dc=1)
    state = folded(query, [second_c, *a_y[:2]], state)
    last = [a_y[2], b_x]
    last_c = by_xor(jnp.concatenate(last, axis=0), dc=1)
    state = folded(query, [third_c, *last], state)
    state = folded(query, [last_c], state)

    parts = messages(state, slots)
    parts = [
        parts[0],
        by_xor(parts[1], dx=1),
        by_xor(parts[2], dz=1),
        by_xor(parts[3], dx=1, dz=1),
    ]
    return combined(parts, suffix, request_row)


def solution(mesh):
    placed = (
        P(AXES, None),
        P(AXES, None),
        P(AXES, None),
        P(AXES, None),
        P(AXES, None),
        P(AXES),
    )
    return jax.shard_map(
        per_device, mesh=mesh, in_specs=placed, out_specs=P(AXES, None), check_vma=False
    )
```

time: 1010 us -> 133 us (0.13)
  waiting for transfers between devices: 840 us -> 35.2 us
  matrix products: 92.4 us -> 0 us
  Pallas kernels: 0 us -> 55.5 us
  other arithmetic: 53.4 us -> 1.03 us
  starting transfers between devices: 0.04 us -> 34.9 us
  between operations: 13.5 us -> 0.2 us
    all_gather x2 -> x0, waiting for transfers between devices: 838 us -> none  [the longest x1 419 us: prefix_states(): lax.all_gather(prefix_keys, ('ctx', 'req'), axis=0, tiled=True)]
    dot_general x34 -> x0, matrix products: 92.4 us -> none  [the longest x16 58.9 us: one_block(): jnp.einsum('rhd,nd->rhn', query_block, key_block, preferred_element_type=...]
    pallas_call x0 -> x9, Pallas kernels: none -> 55.5 us  [the longest x5 44.1 us: folded(): pl.pallas_call(lambda *refs: fold_kernel(len(pieces), first, *refs), out_...]
    reduce_sum x17 -> x0, other arithmetic: 50.8 us -> none  [the longest x16 50.6 us: one_block(): mass_total = mass_total * shrink + jnp.sum(weights, axis=-1)]
    ppermute x0 -> x21, waiting for transfers between devices: none -> 35.2 us  [moved(): return lax.ppermute(array, AXES, sorted(pairs))]
    ppermute x0 -> x21, starting transfers between devices: none -> 34.9 us  [moved(): return lax.ppermute(array, AXES, sorted(pairs))]
  transfers between devices with their start and end apart: 2 -> 21, of which waited for: 2 -> 11; matrix products, arithmetic and copies ran while one was open for 0% -> 0% of each run, Pallas kernels for 0% -> 31%
where the time goes in v1:
time: 133 us; the launch traced here: 131 us
  Pallas kernels  55.5 us (42%)
  waiting for transfers between devices  35.2 us (26%)
  starting transfers between devices  34.9 us (26%)
  local copies, waits for them, and re-layouts  4.76 us (4%)
    pallas_call x5, Pallas kernels, folded(): pl.pallas_call(lambda *refs: fold_kernel(len(pieces), first, *refs), out_...  44.1 us
    ppermute x21, waiting for transfers between devices, moved(): return lax.ppermute(array, AXES, sorted(pairs))  35.2 us
    ppermute x21, starting transfers between devices, moved(): return lax.ppermute(array, AXES, sorted(pairs))  34.9 us
    unnamed x43, local copies, waits for them, and re-layouts  4.72 us
    pallas_call x1, Pallas kernels, suffix_part(): pl.pallas_call(suffix_kernel, out_shape=(shape, shape), in_specs=[VMEM] *...  3.56 us
    pallas_call x1, Pallas kernels, messages(): pl.pallas_call(message_kernel, out_shape=tuple((jax.ShapeDtypeStruct((slo...  3.01 us
  transfers between devices with their start and end apart: 21, of which 11 were waited for; matrix products, arithmetic and copies ran while one was open for 0% of the time, Pallas kernels for 31%

profile of v1, /device:TPU:32, one launch (start us, length us, event | category | flops | bytes accessed | tf_op | source)
XLA Modules:
  0.0 131.5 jit_solution(8391061965942495232)
XLA Ops:
  0.8 3.3 %collective-permute-start.6 = (bf16[1,256,128]{2,1,0:T(8,128)(2,1)S(1)}, bf16[1,256,128]{2,1,0:T(8,128)(2,1)S(1)}, u32[]{:S(2)}, u32[]{:S(2)}) collective-permute-start(bf16[1,256,128]{2,1,0:T(8,128)(2,1)S(1)} %maximum_bitcast_fusion), channel_id=1, source_target_pairs={{0,4},{1,5},{2,6},{3,7},{4,8},{5,9},{6,10},{7,11},{8,12},{9,13},{1... | collective-permute-start | bytes 196616 | tf_op jit(solution)/shard_map/ppermute | solution.py:33
  4.1 2.2 %collective-permute-start.7 = (bf16[1,256,128]{2,1,0:T(8,128)(2,1)S(1)}, bf16[1,256,128]{2,1,0:T(8,128)(2,1)S(1)}, u32[]{:S(2)}, u32[]{:S(2)}) collective-permute-start(bf16[1,256,128]{2,1,0:T(8,128)(2,1)S(1)} %maximum_bitcast_fusion), channel_id=1, source_target_pairs={{0,12},{1,13},{2,14},{3,15},{4,0},{5,1},{6,2},{7,3},{8,4},{9,5},{1... | collective-permute-start | bytes 196616 | tf_op jit(solution)/shard_map/ppermute | solution.py:33
  6.3 3.4 %collective-permute-done.6 = bf16[1,256,128]{2,1,0:T(8,128)(2,1)S(1)} collective-permute-done((bf16[1,256,128]{2,1,0:T(8,128)(2,1)S(1)}, bf16[1,256,128]{2,1,0:T(8,128)(2,1)S(1)}, u32[]{:S(2)}, u32[]{:S(2)}) %collective-permute-start.6) | collective-permute-done | bytes 65568 | tf_op jit(solution)/shard_map/ppermute | solution.py:33
  9.9 1.7 %collective-permute-start.8 = (bf16[2,256,128]{2,1,0:T(8,128)(2,1)S(1)}, bf16[2,256,128]{2,1,0:T(8,128)(2,1)S(1)}, u32[]{:S(2)}, u32[]{:S(2)}) collective-permute-start(bf16[2,256,128]{2,1,0:T(8,128)(2,1)S(1)} %get-tuple-element.39), channel_id=1, source_target_pairs={{0,32},{1,33},{2,34},{3,35},{4,36},{5,37},{6,38},{7,39},{8,40},{9,... | collective-permute-start | bytes 393224 | tf_op jit(solution)/shard_map/ppermute | solution.py:33
  11.6 1.7 %collective-permute-start.9 = (bf16[2,256,128]{2,1,0:T(8,128)(2,1)S(1)}, bf16[2,256,128]{2,1,0:T(8,128)(2,1)S(1)}, u32[]{:S(2)}, u32[]{:S(2)}) collective-permute-start(bf16[2,256,128]{2,1,0:T(8,128)(2,1)S(1)} %get-tuple-element.39), channel_id=1, source_target_pairs={{0,96},{1,97},{2,98},{3,99},{4,100},{5,101},{6,102},{7,103},{8,104... | collective-permute-start | bytes 393224 | tf_op jit(solution)/shard_map/ppermute | solution.py:33
  13.2 4.9 %collective-permute-start.3 = (bf16[1,256,128]{2,1,0:T(8,128)(2,1)S(1)}, bf16[1,256,128]{2,1,0:T(8,128)(2,1)S(1)}, u32[]{:S(2)}, u32[]{:S(2)}) collective-permute-start(bf16[1,256,128]{2,1,0:T(8,128)(2,1)S(1)} %maximum_bitcast_fusion), channel_id=1, source_target_pairs={{0,8},{1,9},{2,10},{3,11},{4,12},{5,13},{6,14},{7,15},{8,0},{9,1},... | collective-permute-start | bytes 196616 | tf_op jit(solution)/shard_map/ppermute | solution.py:33
  18.2 2.0 %collective-permute-start.10 = (bf16[2,256,128]{2,1,0:T(8,128)(2,1)S(1)}, bf16[2,256,128]{2,1,0:T(8,128)(2,1)S(1)}, u32[]{:S(2)}, u32[]{:S(2)}) collective-permute-start(bf16[2,256,128]{2,1,0:T(8,128)(2,1)S(1)} %get-tuple-element.39), channel_id=1, source_target_pairs={{0,64},{1,65},{2,66},{3,67},{4,68},{5,69},{6,70},{7,71},{8,72},{9,... | collective-permute-start | bytes 393224 | tf_op jit(solution)/shard_map/ppermute | solution.py:33
  20.2 4.4 %collective-permute-done.10.refs_5_ = bf16[2,256,128]{2,1,0:T(8,128)(2,1)S(1)} collective-permute-done((bf16[2,256,128]{2,1,0:T(8,128)(2,1)S(1)}, bf16[2,256,128]{2,1,0:T(8,128)(2,1)S(1)}, u32[]{:S(2)}, u32[]{:S(2)}) %collective-permute-start.10) | collective-permute-done | bytes 131104 | tf_op jit(solution)/shard_map/ppermute | solution.py:33
  24.6 3.1 %collective-permute-start.11 = (bf16[8,256,128]{2,1,0:T(8,128)(2,1)S(1)}, bf16[8,256,128]{2,1,0:T(8,128)(2,1)S(1)}, u32[]{:S(2)}, u32[]{:S(2)}) collective-permute-start(bf16[8,256,128]{2,1,0:T(8,128)(2,1)S(1)} %constant_dynamic-update-slice_fusion.2), channel_id=1, source_target_pairs={{0,16},{1,17},{2,18},{3,19},{4,20},{5,21},{6,22},{7,23},{8,24},{9,... | collective-permute-start | bytes 1572872 | tf_op jit(solution)/shard_map/ppermute | solution.py:33
  28.4 11.1 %collective-permute-done.4.refs_2_ = bf16[2,256,128]{2,1,0:T(8,128)(2,1)S(1)} collective-permute-done((bf16[2,256,128]{2,1,0:T(8,128)(2,1)S(1)}, bf16[2,256,128]{2,1,0:T(8,128)(2,1)S(1)}, u32[]{:S(2)}, u32[]{:S(2)}) %collective-permute-start.4) | collective-permute-done | bytes 131104 | tf_op jit(solution)/shard_map/ppermute | solution.py:33
  39.5 1.9 %collective-permute-start.5 = (bf16[4,256,128]{2,1,0:T(8,128)(2,1)S(1)}, bf16[4,256,128]{2,1,0:T(8,128)(2,1)S(1)}, u32[]{:S(2)}, u32[]{:S(2)}) collective-permute-start(bf16[4,256,128]{2,1,0:T(8,128)(2,1)S(1)} %get-tuple-element.38), channel_id=1, source_target_pairs={{0,64},{1,65},{2,66},{3,67},{4,68},{5,69},{6,70},{7,71},{8,72},{9,... | collective-permute-start | bytes 786440 | tf_op jit(solution)/shard_map/ppermute | solution.py:33
  42.1 2.6 %collective-permute-start.14 = (bf16[4,256,128]{2,1,0:T(8,128)(2,1)S(1)}, bf16[4,256,128]{2,1,0:T(8,128)(2,1)S(1)}, u32[]{:S(2)}, u32[]{:S(2)}) collective-permute-start(bf16[4,256,128]{2,1,0:T(8,128)(2,1)S(1)} %get-tuple-element.38), channel_id=1, source_target_pairs={{0,96},{1,97},{2,98},{3,99},{4,100},{5,101},{6,102},{7,103},{8,104... | collective-permute-start | bytes 786440 | tf_op jit(solution)/shard_map/ppermute | solution.py:33
  44.7 3.3 %collective-permute-done.5.refs_2_ = bf16[4,256,128]{2,1,0:T(8,128)(2,1)S(1)} collective-permute-done((bf16[4,256,128]{2,1,0:T(8,128)(2,1)S(1)}, bf16[4,256,128]{2,1,0:T(8,128)(2,1)S(1)}, u32[]{:S(2)}, u32[]{:S(2)}) %collective-permute-start.5) | collective-permute-done | bytes 262176 | tf_op jit(solution)/shard_map/ppermute | solution.py:33
  48.8 1.8 %collective-permute-done.13.refs_2_ = bf16[4,256,128]{2,1,0:T(8,128)(2,1)S(1)} collective-permute-done((bf16[4,256,128]{2,1,0:T(8,128)(2,1)S(1)}, bf16[4,256,128]{2,1,0:T(8,128)(2,1)S(1)}, u32[]{:S(2)}, u32[]{:S(2)}) %collective-permute-start.13) | collective-permute-done | bytes 262176 | tf_op jit(solution)/shard_map/ppermute | solution.py:33
  50.9 1.6 %collective-permute-start = (bf16[64,1024]{1,0:T(8,128)(2,1)S(1)}, bf16[64,1024]{1,0:T(8,128)(2,1)S(1)}, u32[]{:S(2)}, u32[]{:S(2)}) collective-permute-start(bf16[64,1024]{1,0:T(8,128)(2,1)S(1)} %copy-done.11), channel_id=1, source_target_pairs={{0,128},{1,129},{2,130},{3,131},{4,132},{5,133},{6,134},{7,135},{8... | collective-permute-start | bytes 393224 | tf_op jit(solution)/shard_map/ppermute | solution.py:33
  52.4 2.7 %collective-permute-start.1 = (bf16[64,1024]{1,0:T(8,128)(2,1)S(1)}, bf16[64,1024]{1,0:T(8,128)(2,1)S(1)}, u32[]{:S(2)}, u32[]{:S(2)}) collective-permute-start(bf16[64,1024]{1,0:T(8,128)(2,1)S(1)} %copy-done.11), channel_id=1, source_target_pairs={{0,2},{1,3},{2,0},{3,1},{4,6},{5,7},{6,4},{7,5},{8,10},{9,11},{10,... | collective-permute-start | bytes 393224 | tf_op jit(solution)/shard_map/ppermute | solution.py:33
  55.2 1.6 %collective-permute-done.refs_1_ = bf16[64,1024]{1,0:T(8,128)(2,1)S(1)} collective-permute-done((bf16[64,1024]{1,0:T(8,128)(2,1)S(1)}, bf16[64,1024]{1,0:T(8,128)(2,1)S(1)}, u32[]{:S(2)}, u32[]{:S(2)}) %collective-permute-start) | collective-permute-done | bytes 131104 | tf_op jit(solution)/shard_map/ppermute | solution.py:33
  56.8 2.2 %collective-permute-done.1.refs_2_ = bf16[64,1024]{1,0:T(8,128)(2,1)S(1)} collective-permute-done((bf16[64,1024]{1,0:T(8,128)(2,1)S(1)}, bf16[64,1024]{1,0:T(8,128)(2,1)S(1)}, u32[]{:S(2)}, u32[]{:S(2)}) %collective-permute-start.1) | collective-permute-done | bytes 131104 | tf_op jit(solution)/shard_map/ppermute | solution.py:33
  59.0 1.7 %collective-permute-start.2 = (bf16[64,1024]{1,0:T(8,128)(2,1)S(1)}, bf16[64,1024]{1,0:T(8,128)(2,1)S(1)}, u32[]{:S(2)}, u32[]{:S(2)}) collective-permute-start(bf16[64,1024]{1,0:T(8,128)(2,1)S(1)} %copy-done.11), channel_id=1, source_target_pairs={{0,130},{1,131},{2,128},{3,129},{4,134},{5,135},{6,132},{7,133},{8... | collective-permute-start | bytes 393224 | tf_op jit(solution)/shard_map/ppermute | solution.py:33
  60.7 4.2 %collective-permute-done.2.refs_3_ = bf16[64,1024]{1,0:T(8,128)(2,1)S(1)} collective-permute-done((bf16[64,1024]{1,0:T(8,128)(2,1)S(1)}, bf16[64,1024]{1,0:T(8,128)(2,1)S(1)}, u32[]{:S(2)}, u32[]{:S(2)}) %collective-permute-start.2) | collective-permute-done | bytes 131104 | tf_op jit(solution)/shard_map/ppermute | solution.py:33
  65.6 2.3 %shard_map.64.refs_0_ = bf16[2048,256]{1,0:T(8,128)(2,1)} custom-call(bf16[64,1024]{1,0:T(8,128)(2,1)} %queries.1, bf16[64,1024]{1,0:T(8,128)(2,1)} %copy-done.17, bf16[64,1024]{1,0:T(8,128)(2,1)} %copy-done.18, bf16[64,1024]{1,0:T(8,128)(2,1)} %copy-done.19), custom_call_target="tpu_custom_call" | custom-call | tf_op jit(solution)/shard_map/pallas_call | solution.py:71
  67.9 4.9 %shard_map.65 = (f32[2048,256]{1,0:T(8,128)}, f32[2048,128]{1,0:T(8,128)}) custom-call(bf16[2048,256]{1,0:T(8,128)(2,1)} %shard_map.64.refs_0_, bf16[4,256,128]{2,1,0:T(8,128)(2,1)} %copy-done.5), custom_call_target="tpu_custom_call" | custom-call | tf_op jit(solution)/shard_map/pallas_call | solution.py:147
  73.5 8.7 %shard_map.66 = (f32[2048,256]{1,0:T(8,128)}, f32[2048,128]{1,0:T(8,128)}) custom-call(bf16[2048,256]{1,0:T(8,128)(2,1)} %shard_map.64.refs_0_, bf16[4,256,128]{2,1,0:T(8,128)(2,1)} %copy-done.13, bf16[2,256,128]{2,1,0:T(8,128)(2,1)} %copy-done.1, bf16[2,256,128]{2,1,0:T(8,128)(2,1)} %copy-done.2, ...), custom_call_target="tpu_custom_call", output_to_operand_aliasing={{0}: (6, {}), {1}: (7, {})} | custom-call | tf_op jit(solution)/shard_map/pallas_call | solution.py:147
  83.1 10.1 %shard_map.67 = (f32[2048,256]{1,0:T(8,128)}, f32[2048,128]{1,0:T(8,128)}) custom-call(bf16[2048,256]{1,0:T(8,128)(2,1)} %shard_map.64.refs_0_, bf16[8,256,128]{2,1,0:T(8,128)(2,1)} %copy-done.10, bf16[4,256,128]{2,1,0:T(8,128)(2,1)} %copy-done.6, bf16[4,256,128]{2,1,0:T(8,128)(2,1)} %copy-done.7, ...), custom_call_target="tpu_custom_call", output_to_operand_aliasing={{0}: (4, {}), {1}: (5, {})} | custom-call | tf_op jit(solution)/shard_map/pallas_call | solution.py:147
  94.0 11.5 %shard_map.68 = (f32[2048,256]{1,0:T(8,128)}, f32[2048,128]{1,0:T(8,128)}) custom-call(bf16[2048,256]{1,0:T(8,128)(2,1)} %shard_map.64.refs_0_, bf16[8,256,128]{2,1,0:T(8,128)(2,1)} %copy-done.12, bf16[4,256,128]{2,1,0:T(8,128)(2,1)} %copy-done.8, bf16[8,256,128]{2,1,0:T(8,128)(2,1)} %copy-done, ...), custom_call_target="tpu_custom_call", output_to_operand_aliasing={{0}: (4, {}), {1}: (5, {})} | custom-call | tf_op jit(solution)/shard_map/pallas_call | solution.py:147
  105.5 0.9 copy-done.9
  106.4 8.9 %shard_map.69 = (f32[2048,256]{1,0:T(8,128)}, f32[2048,128]{1,0:T(8,128)}) custom-call(bf16[2048,256]{1,0:T(8,128)(2,1)} %shard_map.64.refs_0_, bf16[12,256,128]{2,1,0:T(8,128)(2,1)} %copy-done.9, f32[2048,256]{1,0:T(8,128)} %get-tuple-element.27.refs_2_, f32[2048,128]{1,0:T(8,128)} %get-tuple-element.28.refs_3_), custom_call_target="tpu_custom_call", output_to_operand_aliasing={{0}: (2, {}), {1}: (3, {})} | custom-call | tf_op jit(solution)/shard_map/pallas_call | solution.py:147
  115.4 3.0 %shard_map.70 = (bf16[64,1152]{1,0:T(8,128)(2,1)}, bf16[64,1152]{1,0:T(8,128)(2,1)}, bf16[64,1152]{1,0:T(8,128)(2,1)}, bf16[64,1152]{1,0:T(8,128)(2,1)}) custom-call(f32[2048,256]{1,0:T(8,128)} %get-tuple-element.29.total, f32[2048,128]{1,0:T(8,128)} %get-tuple-element.30.peak), custom_call_target="tpu_custom_call" | custom-call | tf_op jit(solution)/shard_map/pallas_call | solution.py:182
  118.9 2.4 %collective-permute-start.19 = (bf16[64,1152]{1,0:T(8,128)(2,1)}, bf16[64,1152]{1,0:T(8,128)(2,1)S(1)}, u32[]{:S(2)}, u32[]{:S(2)}) collective-permute-start(bf16[64,1152]{1,0:T(8,128)(2,1)} %get-tuple-element.33), channel_id=1, source_target_pairs={{0,2},{1,3},{2,0},{3,1},{4,6},{5,7},{6,4},{7,5},{8,10},{9,11},{10,... | collective-permute-start | bytes 442376 | tf_op jit(solution)/shard_map/ppermute | solution.py:33
  121.8 3.6 %shard_map.71 = (f32[512,128]{1,0:T(8,128)}, f32[512,128]{1,0:T(8,128)}) custom-call(bf16[64,1024]{1,0:T(8,128)(2,1)} %queries.1, bf16[64,128]{1,0:T(8,128)(2,1)} %key_rows.1, bf16[64,128]{1,0:T(8,128)(2,1)} %value_rows.1, s32[1,64]{1,0:T(1,128)} %bitcast.3), custom_call_target="tpu_custom_call" | custom-call | tf_op jit(solution)/shard_map/pallas_call | solution.py:221
  126.2 2.1 %collective-permute-done.20.refs_3_ = bf16[64,1152]{1,0:T(8,128)(2,1)S(1)} collective-permute-done((bf16[64,1152]{1,0:T(8,128)(2,1)}, bf16[64,1152]{1,0:T(8,128)(2,1)S(1)}, u32[]{:S(2)}, u32[]{:S(2)}) %collective-permute-start.20) | collective-permute-done | bytes 147488 | tf_op jit(solution)/shard_map/ppermute | solution.py:33
  129.0 2.5 %shard_map.72 = bf16[64,1024]{1,0:T(8,128)(2,1)} custom-call(bf16[64,1152]{1,0:T(8,128)(2,1)} %get-tuple-element.31.refs_0_, bf16[64,1152]{1,0:T(8,128)(2,1)} %copy-done.14, bf16[64,1152]{1,0:T(8,128)(2,1)} %copy-done.15, bf16[64,1152]{1,0:T(8,128)(2,1)} %copy-done.16, f32[512,128]{1,0:T(8,128)} %get-tuple-element.35.refs_4_, ...), custom_call_target="tpu_custom_call" | custom-call | tf_op jit(solution)/shard_map/pallas_call | solution.py:260
  (70 shorter events, 9.0 us)
Async XLA Ops:
  0.8 8.9 %collective-permute-start.6 = (bf16[1,256,128]{2,1,0:T(8,128)(2,1)S(1)}, bf16[1,256,128]{2,1,0:T(8,128)(2,1)S(1)}, u32[]{:S(2)}, u32[]{:S(2)}) collective-permute-start(bf16[1,256,128]{2,1,0:T(8,128)(2,1)S(1)} %maximum_bitcast_fusion), channel_id=1, source_target_pairs={{0,4},{1,5},{2,6},{3,7},{4,8},{5,9},{6,10},{7,11},{8,12},{9,13},{1... | collective-permute-start | bytes 196616 | tf_op jit(solution)/shard_map/ppermute | solution.py:33
  4.1 5.8 %collective-permute-start.7 = (bf16[1,256,128]{2,1,0:T(8,128)(2,1)S(1)}, bf16[1,256,128]{2,1,0:T(8,128)(2,1)S(1)}, u32[]{:S(2)}, u32[]{:S(2)}) collective-permute-start(bf16[1,256,128]{2,1,0:T(8,128)(2,1)S(1)} %maximum_bitcast_fusion), channel_id=1, source_target_pairs={{0,12},{1,13},{2,14},{3,15},{4,0},{5,1},{6,2},{7,3},{8,4},{9,5},{1... | collective-permute-start | bytes 196616 | tf_op jit(solution)/shard_map/ppermute | solution.py:33
  9.9 10.2 %collective-permute-start.8 = (bf16[2,256,128]{2,1,0:T(8,128)(2,1)S(1)}, bf16[2,256,128]{2,1,0:T(8,128)(2,1)S(1)}, u32[]{:S(2)}, u32[]{:S(2)}) collective-permute-start(bf16[2,256,128]{2,1,0:T(8,128)(2,1)S(1)} %get-tuple-element.39), channel_id=1, source_target_pairs={{0,32},{1,33},{2,34},{3,35},{4,36},{5,37},{6,38},{7,39},{8,40},{9,... | collective-permute-start | bytes 393224 | tf_op jit(solution)/shard_map/ppermute | solution.py:33
  11.6 8.6 %collective-permute-start.9 = (bf16[2,256,128]{2,1,0:T(8,128)(2,1)S(1)}, bf16[2,256,128]{2,1,0:T(8,128)(2,1)S(1)}, u32[]{:S(2)}, u32[]{:S(2)}) collective-permute-start(bf16[2,256,128]{2,1,0:T(8,128)(2,1)S(1)} %get-tuple-element.39), channel_id=1, source_target_pairs={{0,96},{1,97},{2,98},{3,99},{4,100},{5,101},{6,102},{7,103},{8,104... | collective-permute-start | bytes 393224 | tf_op jit(solution)/shard_map/ppermute | solution.py:33
  13.2 14.5 %collective-permute-start.3 = (bf16[1,256,128]{2,1,0:T(8,128)(2,1)S(1)}, bf16[1,256,128]{2,1,0:T(8,128)(2,1)S(1)}, u32[]{:S(2)}, u32[]{:S(2)}) collective-permute-start(bf16[1,256,128]{2,1,0:T(8,128)(2,1)S(1)} %maximum_bitcast_fusion), channel_id=1, source_target_pairs={{0,8},{1,9},{2,10},{3,11},{4,12},{5,13},{6,14},{7,15},{8,0},{9,1},... | collective-permute-start | bytes 196616 | tf_op jit(solution)/shard_map/ppermute | solution.py:33
  18.2 6.5 %collective-permute-start.10 = (bf16[2,256,128]{2,1,0:T(8,128)(2,1)S(1)}, bf16[2,256,128]{2,1,0:T(8,128)(2,1)S(1)}, u32[]{:S(2)}, u32[]{:S(2)}) collective-permute-start(bf16[2,256,128]{2,1,0:T(8,128)(2,1)S(1)} %get-tuple-element.39), channel_id=1, source_target_pairs={{0,64},{1,65},{2,66},{3,67},{4,68},{5,69},{6,70},{7,71},{8,72},{9,... | collective-permute-start | bytes 393224 | tf_op jit(solution)/shard_map/ppermute | solution.py:33
  20.1 28.1 %copy-start.2 = (bf16[2,256,128]{2,1,0:T(8,128)(2,1)}, bf16[2,256,128]{2,1,0:T(8,128)(2,1)S(1)}, u32[]{:S(2)}) copy-start(bf16[2,256,128]{2,1,0:T(8,128)(2,1)S(1)} %collective-permute-done.8.refs_3_) | copy-start | bytes 393220
  20.2 28.1 %copy-start.3 = (bf16[2,256,128]{2,1,0:T(8,128)(2,1)}, bf16[2,256,128]{2,1,0:T(8,128)(2,1)S(1)}, u32[]{:S(2)}) copy-start(bf16[2,256,128]{2,1,0:T(8,128)(2,1)S(1)} %collective-permute-done.9.refs_4_) | copy-start | bytes 393220
  24.6 26.1 %copy-start.4 = (bf16[2,256,128]{2,1,0:T(8,128)(2,1)}, bf16[2,256,128]{2,1,0:T(8,128)(2,1)S(1)}, u32[]{:S(2)}) copy-start(bf16[2,256,128]{2,1,0:T(8,128)(2,1)S(1)} %collective-permute-done.10.refs_5_) | copy-start | bytes 393220
  24.6 23.3 %collective-permute-start.11 = (bf16[8,256,128]{2,1,0:T(8,128)(2,1)S(1)}, bf16[8,256,128]{2,1,0:T(8,128)(2,1)S(1)}, u32[]{:S(2)}, u32[]{:S(2)}) collective-permute-start(bf16[8,256,128]{2,1,0:T(8,128)(2,1)S(1)} %constant_dynamic-update-slice_fusion.2), channel_id=1, source_target_pairs={{0,16},{1,17},{2,18},{3,19},{4,20},{5,21},{6,22},{7,23},{8,24},{9,... | collective-permute-start | bytes 1572872 | tf_op jit(solution)/shard_map/ppermute | solution.py:33
  27.8 23.1 %copy-start.11 = (bf16[64,1024]{1,0:T(8,128)(2,1)S(1)}, bf16[64,1024]{1,0:T(8,128)(2,1)}, u32[]{:S(2)}) copy-start(bf16[64,1024]{1,0:T(8,128)(2,1)} %queries.1) | copy-start | bytes 393220
  27.8 11.7 %collective-permute-start.4 = (bf16[2,256,128]{2,1,0:T(8,128)(2,1)S(1)}, bf16[2,256,128]{2,1,0:T(8,128)(2,1)S(1)}, u32[]{:S(2)}, u32[]{:S(2)}) collective-permute-start(bf16[2,256,128]{2,1,0:T(8,128)(2,1)S(1)} %pad_maximum_fusion.6), channel_id=1, source_target_pairs={{0,16},{1,17},{2,18},{3,19},{4,20},{5,21},{6,22},{7,23},{8,24},{9,... | collective-permute-start | bytes 393224 | tf_op jit(solution)/shard_map/ppermute | solution.py:33
  39.5 11.3 %copy-start.1 = (bf16[2,256,128]{2,1,0:T(8,128)(2,1)}, bf16[2,256,128]{2,1,0:T(8,128)(2,1)S(1)}, u32[]{:S(2)}) copy-start(bf16[2,256,128]{2,1,0:T(8,128)(2,1)S(1)} %collective-permute-done.4.refs_2_) | copy-start | bytes 393220
  39.5 28.3 %copy-start.5 = (bf16[4,256,128]{2,1,0:T(8,128)(2,1)}, bf16[4,256,128]{2,1,0:T(8,128)(2,1)S(1)}, u32[]{:S(2)}) copy-start(bf16[4,256,128]{2,1,0:T(8,128)(2,1)S(1)} %get-tuple-element.37.refs_1_) | copy-start | bytes 786436
  39.5 8.4 %collective-permute-start.5 = (bf16[4,256,128]{2,1,0:T(8,128)(2,1)S(1)}, bf16[4,256,128]{2,1,0:T(8,128)(2,1)S(1)}, u32[]{:S(2)}, u32[]{:S(2)}) collective-permute-start(bf16[4,256,128]{2,1,0:T(8,128)(2,1)S(1)} %get-tuple-element.38), channel_id=1, source_target_pairs={{0,64},{1,65},{2,66},{3,67},{4,68},{5,69},{6,70},{7,71},{8,72},{9,... | collective-permute-start | bytes 786440 | tf_op jit(solution)/shard_map/ppermute | solution.py:33
  41.5 9.2 %collective-permute-start.13 = (bf16[4,256,128]{2,1,0:T(8,128)(2,1)S(1)}, bf16[4,256,128]{2,1,0:T(8,128)(2,1)S(1)}, u32[]{:S(2)}, u32[]{:S(2)}) collective-permute-start(bf16[4,256,128]{2,1,0:T(8,128)(2,1)S(1)} %get-tuple-element.38), channel_id=1, source_target_pairs={{0,32},{1,33},{2,34},{3,35},{4,36},{5,37},{6,38},{7,39},{8,40},{9,... | collective-permute-start | bytes 786440 | tf_op jit(solution)/shard_map/ppermute | solution.py:33
  42.1 8.5 %collective-permute-start.14 = (bf16[4,256,128]{2,1,0:T(8,128)(2,1)S(1)}, bf16[4,256,128]{2,1,0:T(8,128)(2,1)S(1)}, u32[]{:S(2)}, u32[]{:S(2)}) collective-permute-start(bf16[4,256,128]{2,1,0:T(8,128)(2,1)S(1)} %get-tuple-element.38), channel_id=1, source_target_pairs={{0,96},{1,97},{2,98},{3,99},{4,100},{5,101},{6,102},{7,103},{8,104... | collective-permute-start | bytes 786440 | tf_op jit(solution)/shard_map/ppermute | solution.py:33
  48.0 19.9 %copy-start.8 = (bf16[4,256,128]{2,1,0:T(8,128)(2,1)}, bf16[4,256,128]{2,1,0:T(8,128)(2,1)S(1)}, u32[]{:S(2)}) copy-start(bf16[4,256,128]{2,1,0:T(8,128)(2,1)S(1)} %collective-permute-done.5.refs_2_) | copy-start | bytes 786436
  48.0 19.9 %copy-start = (bf16[8,256,128]{2,1,0:T(8,128)(2,1)}, bf16[8,256,128]{2,1,0:T(8,128)(2,1)S(1)}, u32[]{:S(2)}) copy-start(bf16[8,256,128]{2,1,0:T(8,128)(2,1)S(1)} %collective-permute-done.11.refs_3_) | copy-start | bytes 1572868
  48.0 57.5 %collective-permute-start.12 = (bf16[12,256,128]{2,1,0:T(8,128)(2,1)S(1)}, bf16[12,256,128]{2,1,0:T(8,128)(2,1)S(1)}, u32[]{:S(2)}, u32[]{:S(2)}) collective-permute-start(bf16[12,256,128]{2,1,0:T(8,128)(2,1)S(1)} %pad_maximum_fusion), channel_id=1, source_target_pairs={{0,1},{1,0},{2,3},{3,2},{4,5},{5,4},{6,7},{7,6},{8,9},{9,8},{10,11... | collective-permute-start | bytes 2359304 | tf_op jit(solution)/shard_map/ppermute | solution.py:33
  48.2 34.0 %collective-permute-start.16 = (bf16[8,256,128]{2,1,0:T(8,128)(2,1)S(1)}, bf16[8,256,128]{2,1,0:T(8,128)(2,1)S(1)}, u32[]{:S(2)}, u32[]{:S(2)}) collective-permute-start(bf16[8,256,128]{2,1,0:T(8,128)(2,1)S(1)} %pad_maximum_fusion.2), channel_id=1, source_target_pairs={{0,1},{1,0},{2,3},{3,2},{4,5},{5,4},{6,7},{7,6},{8,9},{9,8},{10,11... | collective-permute-start | bytes 1572872 | tf_op jit(solution)/shard_map/ppermute | solution.py:33
  50.7 31.5 %copy-start.6 = (bf16[4,256,128]{2,1,0:T(8,128)(2,1)}, bf16[4,256,128]{2,1,0:T(8,128)(2,1)S(1)}, u32[]{:S(2)}) copy-start(bf16[4,256,128]{2,1,0:T(8,128)(2,1)S(1)} %collective-permute-done.13.refs_2_) | copy-start | bytes 786436
  50.7 31.5 %copy-start.7 = (bf16[4,256,128]{2,1,0:T(8,128)(2,1)}, bf16[4,256,128]{2,1,0:T(8,128)(2,1)S(1)}, u32[]{:S(2)}) copy-start(bf16[4,256,128]{2,1,0:T(8,128)(2,1)S(1)} %collective-permute-done.14.refs_3_) | copy-start | bytes 786436
  50.7 42.4 %collective-permute-start.15 = (bf16[8,256,128]{2,1,0:T(8,128)(2,1)S(1)}, bf16[8,256,128]{2,1,0:T(8,128)(2,1)S(1)}, u32[]{:S(2)}, u32[]{:S(2)}) collective-permute-start(bf16[8,256,128]{2,1,0:T(8,128)(2,1)S(1)} %pad_maximum_fusion.1), channel_id=1, source_target_pairs={{0,1},{1,0},{2,3},{3,2},{4,5},{5,4},{6,7},{7,6},{8,9},{9,8},{10,11... | collective-permute-start | bytes 1572872 | tf_op jit(solution)/shard_map/ppermute | solution.py:33
  50.9 5.9 %collective-permute-start = (bf16[64,1024]{1,0:T(8,128)(2,1)S(1)}, bf16[64,1024]{1,0:T(8,128)(2,1)S(1)}, u32[]{:S(2)}, u32[]{:S(2)}) collective-permute-start(bf16[64,1024]{1,0:T(8,128)(2,1)S(1)} %copy-done.11), channel_id=1, source_target_pairs={{0,128},{1,129},{2,130},{3,131},{4,132},{5,133},{6,134},{7,135},{8... | collective-permute-start | bytes 393224 | tf_op jit(solution)/shard_map/ppermute | solution.py:33
  52.4 6.5 %collective-permute-start.1 = (bf16[64,1024]{1,0:T(8,128)(2,1)S(1)}, bf16[64,1024]{1,0:T(8,128)(2,1)S(1)}, u32[]{:S(2)}, u32[]{:S(2)}) collective-permute-start(bf16[64,1024]{1,0:T(8,128)(2,1)S(1)} %copy-done.11), channel_id=1, source_target_pairs={{0,2},{1,3},{2,0},{3,1},{4,6},{5,7},{6,4},{7,5},{8,10},{9,11},{10,... | collective-permute-start | bytes 393224 | tf_op jit(solution)/shard_map/ppermute | solution.py:33
  56.8 8.1 %copy-start.17 = (bf16[64,1024]{1,0:T(8,128)(2,1)}, bf16[64,1024]{1,0:T(8,128)(2,1)S(1)}, u32[]{:S(2)}) copy-start(bf16[64,1024]{1,0:T(8,128)(2,1)S(1)} %collective-permute-done.refs_1_) | copy-start | bytes 393220
  56.8 15.9 %collective-permute-start.17 = (bf16[4,256,128]{2,1,0:T(8,128)(2,1)S(1)}, bf16[4,256,128]{2,1,0:T(8,128)(2,1)S(1)}, u32[]{:S(2)}, u32[]{:S(2)}) collective-permute-start(bf16[4,256,128]{2,1,0:T(8,128)(2,1)S(1)} %get-tuple-element.37.refs_1_), channel_id=1, source_target_pairs={{0,1},{1,0},{2,3},{3,2},{4,5},{5,4},{6,7},{7,6},{8,9},{9,8},{10,11... | collective-permute-start | bytes 786440 | tf_op jit(solution)/shard_map/ppermute | solution.py:33
  59.0 5.9 %collective-permute-start.2 = (bf16[64,1024]{1,0:T(8,128)(2,1)S(1)}, bf16[64,1024]{1,0:T(8,128)(2,1)S(1)}, u32[]{:S(2)}, u32[]{:S(2)}) collective-permute-start(bf16[64,1024]{1,0:T(8,128)(2,1)S(1)} %copy-done.11), channel_id=1, source_target_pairs={{0,130},{1,131},{2,128},{3,129},{4,134},{5,135},{6,132},{7,133},{8... | collective-permute-start | bytes 393224 | tf_op jit(solution)/shard_map/ppermute | solution.py:33
  118.4 7.1 %collective-permute-start.18 = (bf16[64,1152]{1,0:T(8,128)(2,1)}, bf16[64,1152]{1,0:T(8,128)(2,1)S(1)}, u32[]{:S(2)}, u32[]{:S(2)}) collective-permute-start(bf16[64,1152]{1,0:T(8,128)(2,1)} %get-tuple-element.32), channel_id=1, source_target_pairs={{0,128},{1,129},{2,130},{3,131},{4,132},{5,133},{6,134},{7,135},{8... | collective-permute-start | bytes 442376 | tf_op jit(solution)/shard_map/ppermute | solution.py:33
  118.9 7.3 %collective-permute-start.19 = (bf16[64,1152]{1,0:T(8,128)(2,1)}, bf16[64,1152]{1,0:T(8,128)(2,1)S(1)}, u32[]{:S(2)}, u32[]{:S(2)}) collective-permute-start(bf16[64,1152]{1,0:T(8,128)(2,1)} %get-tuple-element.33), channel_id=1, source_target_pairs={{0,2},{1,3},{2,0},{3,1},{4,6},{5,7},{6,4},{7,5},{8,10},{9,11},{10,... | collective-permute-start | bytes 442376 | tf_op jit(solution)/shard_map/ppermute | solution.py:33
  121.3 7.1 %collective-permute-start.20 = (bf16[64,1152]{1,0:T(8,128)(2,1)}, bf16[64,1152]{1,0:T(8,128)(2,1)S(1)}, u32[]{:S(2)}, u32[]{:S(2)}) collective-permute-start(bf16[64,1152]{1,0:T(8,128)(2,1)} %get-tuple-element.34), channel_id=1, source_target_pairs={{0,130},{1,131},{2,128},{3,129},{4,134},{5,135},{6,132},{7,133},{8... | collective-permute-start | bytes 442376 | tf_op jit(solution)/shard_map/ppermute | solution.py:33
  (9 other events, 15.7 us)

commit v2 on v1

v2 whole, which is shorter than its diff:
```python
import math

import jax
import jax.numpy as jnp
from jax import lax
from jax.experimental import pallas as pl
from jax.experimental.pallas import tpu as pltpu
from jax.sharding import PartitionSpec as P

H = 8
HD = 128
AXES = ("ctx", "req")
SCALE = 1.4426950408889634 / math.sqrt(HD)
MASKED_SCORE = -1e30
BLOCK = 128
POOL = 4
KEY_TILE = 512
ROW_TILE = 256
MASS_LIMIT = 2.0**100

f32, bf16 = jnp.float32, jnp.bfloat16
VMEM = pl.BlockSpec(memory_space=pltpu.VMEM)
PARAMS = pltpu.CompilerParams(vmem_limit_bytes=24 * 2**20)


def moved(array, place):
    pairs = []
    for x in range(4):
        for y in range(4):
            for z in range(8):
                for c in range(2):
                    pairs.append((linear(x, y, z, c), linear(*place(x, y, z, c))))
    return lax.ppermute(array, AXES, sorted(pairs))


def linear(x, y, z, c):
    return ((x % 2) * 4 + y) * 32 + (x // 2) * 16 + z * 2 + c


def by_xor(array, dx=0, dy=0, dz=0, dc=0):
    return moved(array, lambda x, y, z, c: (x ^ dx, y ^ dy, z ^ dz, c ^ dc))


def by_ring(array, dy=0, dz=0):
    return moved(array, lambda x, y, z, c: (x, (y + dy) % 4, (z + dz) % 8, c))


def wide(column_like, width):
    return jnp.concatenate([column_like] * (width // 128), axis=1)


def spread(column, rows):
    return jnp.broadcast_to(column, (rows, 128))


def prepare(source, out):
    slots = source.shape[0]
    for h in range(H):
        scaled = source[:, h * HD : (h + 1) * HD].astype(f32) * SCALE
        high = scaled.astype(bf16)
        low = (scaled - high.astype(f32)).astype(bf16)
        rows = pl.ds(h * slots, slots)
        out[rows, 0:HD] = high
        out[rows, HD : 2 * HD] = low


def scored(query, keys):
    return lax.dot_general(query, keys, (((1,), (1,)), ((), ())), preferred_element_type=f32)


def request_column(request_row, slots):
    row = lax.broadcasted_iota(jnp.int32, (slots, slots), 0)
    column = lax.broadcasted_iota(jnp.int32, (slots, slots), 1)
    across = jnp.broadcast_to(request_row, (slots, slots))
    return jnp.sum(jnp.where(row == column, across, 0), axis=1, keepdims=True), across, row, column


def cost(rows, keys):
    return pl.CostEstimate(
        flops=8 * rows * keys * HD, transcendentals=rows * keys, bytes_accessed=2048 * rows
    )


def own_kernel(queries, suffix_keys, suffix_values, request, query, quotient, level):
    slots = queries.shape[0]
    prepare(queries, query)
    own, across, row, column = request_column(request[...], slots)
    visible = ((own == across) & (column <= row)).astype(jnp.int32)
    visible = jnp.concatenate([visible] * H, axis=0) == 1
    key_rows = jnp.concatenate([suffix_keys[...]] * 2, axis=1)
    scores = jnp.where(visible, scored(query[...], key_rows), MASKED_SCORE)
    peak = jnp.max(scores, axis=1, keepdims=True)
    weights = jnp.exp2(scores - peak).astype(bf16)
    value_rows = jnp.concatenate([suffix_values[...], jnp.ones((slots, HD), bf16)], axis=1)
    total = jnp.dot(weights, value_rows, preferred_element_type=f32)
    mass = total[:, HD:]
    quotient[...] = total[:, :HD] / mass
    level[...] = spread(peak, H * slots) + jnp.log2(mass)


def own_part(queries, suffix_keys, suffix_values, request_row):
    slots = queries.shape[0]
    shape = jax.ShapeDtypeStruct((H * slots, HD), f32)
    return pl.pallas_call(
        own_kernel,
        out_shape=(jax.ShapeDtypeStruct((H * slots, 2 * HD), bf16), shape, shape),
        in_specs=[VMEM] * 4,
        out_specs=(VMEM,) * 3,
        compiler_params=PARAMS,
        cost_estimate=cost(H * slots, 512),
    )(queries, suffix_keys, suffix_values, request_row)


def load_pieces(pieces, keys, values):
    at = 0
    ones = jnp.ones((BLOCK, HD), bf16)
    for piece in pieces:
        for b in range(piece.shape[0]):
            rows = pl.ds(at, BLOCK)
            key_rows = piece[b, 0:BLOCK, :]
            keys[rows, 0:HD] = key_rows
            keys[rows, HD : 2 * HD] = key_rows
            values[rows, 0:HD] = piece[b, BLOCK : 2 * BLOCK, :]
            values[rows, HD : 2 * HD] = ones
            at += BLOCK
    return at


def first_kernel(*refs):
    query, refs = refs[0], refs[1:]
    others, piece, refs = refs[: POOL - 1], refs[POOL - 1], refs[POOL:]
    prepared, totals, peaks = refs[: POOL - 1], refs[POOL - 1 : 2 * POOL - 1], refs[2 * POOL - 1 : 3 * POOL - 1]
    keys, values = refs[3 * POOL - 1 :]
    key_count = load_pieces([piece], keys, values)
    for source, out in zip(others, prepared):
        prepare(source, out)
    for j, held in enumerate([query, *prepared]):
        for start in range(0, held.shape[0], ROW_TILE):
            rows = pl.ds(start, ROW_TILE)
            scores = scored(held[rows, :], keys[...])
            peak = spread(jnp.max(scores, axis=1, keepdims=True), ROW_TILE)
            weights = jnp.exp2(scores - wide(peak, key_count)).astype(bf16)
            totals[j][rows, :] = jnp.dot(weights, values[...], preferred_element_type=f32)
            peaks[j][rows, :] = peak


def first_fold(query, others, piece):
    rows, key_count = query.shape[0], piece.shape[0] * BLOCK
    shapes = (
        [jax.ShapeDtypeStruct((rows, 2 * HD), bf16)] * (POOL - 1)
        + [jax.ShapeDtypeStruct((rows, 2 * HD), f32)] * POOL
        + [jax.ShapeDtypeStruct((rows, HD), f32)] * POOL
    )
    outs = pl.pallas_call(
        first_kernel,
        out_shape=tuple(shapes),
        in_specs=[VMEM] * (POOL + 1),
        out_specs=(VMEM,) * len(shapes),
        scratch_shapes=[pltpu.VMEM((key_count, 2 * HD), bf16)] * 2,
        compiler_params=PARAMS,
        cost_estimate=cost(POOL * rows, key_count + 512),
    )(query, *others, piece)
    return [query, *outs[: POOL - 1]], outs[POOL - 1 : 2 * POOL - 1], outs[2 * POOL - 1 :]


def add_tile(query, total, peak, keys, values, rows, span):
    weights = jnp.exp2(scored(query[rows, :], keys[span, :]) - wide(peak[rows, :], KEY_TILE))
    total[rows, :] += jnp.dot(weights.astype(bf16), values[span, :], preferred_element_type=f32)


def fold_kernel(piece_count, *refs):
    queries, peaks, refs = refs[:POOL], refs[POOL : 2 * POOL], refs[2 * POOL :]
    pieces, refs = refs[:piece_count], refs[piece_count:]
    totals, (keys, values) = refs[POOL : 2 * POOL], refs[2 * POOL :]
    for held, total in zip(refs[:POOL], totals):
        total[...] = held[...]
    key_count = load_pieces(pieces, keys, values)

    def step(i, _):
        span = pl.ds(pl.multiple_of(i * KEY_TILE, KEY_TILE), KEY_TILE)
        for j in range(POOL):
            for start in range(0, queries[j].shape[0], ROW_TILE):
                add_tile(queries[j], totals[j], peaks[j], keys, values, pl.ds(start, ROW_TILE), span)
        return 0

    lax.fori_loop(0, key_count // KEY_TILE, step, 0)


def folded(queries, peaks, totals, pieces):
    rows = queries[0].shape[0]
    key_count = sum(p.shape[0] for p in pieces) * BLOCK
    assert key_count % KEY_TILE == 0
    at = 2 * POOL + len(pieces)
    return pl.pallas_call(
        lambda *refs: fold_kernel(len(pieces), *refs),
        out_shape=(jax.ShapeDtypeStruct((rows, 2 * HD), f32),) * POOL,
        in_specs=[VMEM] * (at + POOL),
        out_specs=(VMEM,) * POOL,
        scratch_shapes=[pltpu.VMEM((key_count, 2 * HD), bf16)] * 2,
        input_output_aliases={at + j: j for j in range(POOL)},
        compiler_params=PARAMS,
        cost_estimate=cost(POOL * rows, key_count),
    )(*queries, *peaks, *pieces, *totals)


def refold(query, total, peak, blocks, every, semaphore):
    at = 0
    for piece in every:
        copy = pltpu.make_async_copy(piece, blocks.at[pl.ds(at, piece.shape[0])], semaphore)
        copy.start()
        copy.wait()
        at += piece.shape[0]
    total[...] = jnp.zeros_like(total)
    peak[...] = jnp.full(peak.shape, MASKED_SCORE, f32)
    rows = query.shape[0]
    ones = jnp.ones((BLOCK, HD), bf16)

    def step(b, _):
        key_rows = blocks[b, 0:BLOCK, :]
        scores = scored(query[...], jnp.concatenate([key_rows, key_rows], axis=1))
        old = peak[...]
        new = jnp.maximum(old, spread(jnp.max(scores, axis=1, keepdims=True), rows))
        weights = jnp.exp2(scores - new).astype(bf16)
        value_rows = jnp.concatenate([blocks[b, BLOCK : 2 * BLOCK, :], ones], axis=1)
        added = jnp.dot(weights, value_rows, preferred_element_type=f32)
        total[...] = total[...] * wide(jnp.exp2(old - new), 2 * HD) + added
        peak[...] = new
        return 0

    lax.fori_loop(0, at, step, 0)


def last_kernel(piece_count, every_count, *refs):
    query, peak_in, total_in, refs = refs[0], refs[1], refs[2], refs[3:]
    pieces, every, refs = refs[:piece_count], refs[piece_count:][:every_count], refs[piece_count + every_count :]
    out, total, peak, keys, values, blocks, semaphore = refs
    slots = out.shape[0]
    key_count = load_pieces(pieces, keys, values)
    total[...] = total_in[...]
    peak[...] = peak_in[...]
    for key_start in range(0, key_count, KEY_TILE):
        for start in range(0, query.shape[0], ROW_TILE):
            add_tile(query, total, peak, keys, values, pl.ds(start, ROW_TILE), pl.ds(key_start, KEY_TILE))

    @pl.when(jnp.logical_not(jnp.max(total[:, HD:]) < MASS_LIMIT))
    def _():
        refold(query, total, peak, blocks, every, semaphore)

    lane = lax.broadcasted_iota(jnp.int32, (slots, 128), 1)
    packed = jnp.zeros((slots, 128), f32)
    for h in range(H):
        rows = pl.ds(h * slots, slots)
        mass = total[rows, HD : 2 * HD]
        out[:, h * HD : (h + 1) * HD] = (total[rows, 0:HD] / mass).astype(bf16)
        level = peak[rows, :] + jnp.log2(mass)
        one = level.astype(bf16).astype(f32)
        two = (level - one).astype(bf16).astype(f32)
        three = level - one - two
        term = jnp.where(lane % 16 == 0, one, jnp.where(lane % 16 == 1, two, three))
        packed = jnp.where((lane // 16 == h) & (lane % 16 < 3), term, packed)
    out[:, H * HD :] = packed.astype(bf16)


def last_fold(query, peak, total, pieces, every):
    rows = query.shape[0]
    slots = rows // H
    key_count = sum(p.shape[0] for p in pieces) * BLOCK
    block_count = sum(p.shape[0] for p in every)
    return pl.pallas_call(
        lambda *refs: last_kernel(len(pieces), len(every), *refs),
        out_shape=jax.ShapeDtypeStruct((slots, H * HD + 128), bf16),
        in_specs=[VMEM] * (3 + len(pieces)) + [pl.BlockSpec(memory_space=pl.ANY)] * len(every),
        out_specs=VMEM,
        scratch_shapes=[
            pltpu.VMEM((rows, 2 * HD), f32),
            pltpu.VMEM((rows, HD), f32),
            pltpu.VMEM((key_count, 2 * HD), bf16),
            pltpu.VMEM((key_count, 2 * HD), bf16),
            pltpu.VMEM((block_count, 2 * BLOCK, HD), bf16),
            pltpu.SemaphoreType.DMA,
        ],
        compiler_params=PARAMS,
        cost_estimate=cost(rows, key_count),
    )(query, peak, total, *pieces, *every)


def combine_kernel(*refs):
    parts, suffix_quotient, suffix_level, request, out = refs[:-4], *refs[-4:]
    slots = out.shape[0]
    own = request_column(request[...], slots)[0]
    live = jnp.broadcast_to(own < slots, (slots, HD))
    lane = lax.broadcasted_iota(jnp.int32, (128, H * HD), 0)
    column = lax.broadcasted_iota(jnp.int32, (128, H * HD), 1)
    gather = ((lane // 16 == column // HD) & (lane % 16 < 3)).astype(bf16)
    levels = [
        jnp.dot(part[:, H * HD :], gather, preferred_element_type=f32) for part in parts
    ]
    for h in range(H):
        columns = slice(h * HD, (h + 1) * HD)
        rows = pl.ds(h * slots, slots)
        all_levels = [level[:, columns] for level in levels] + [suffix_level[rows, :]]
        all_quotients = [part[:, columns].astype(f32) for part in parts]
        all_quotients.append(suffix_quotient[rows, :])
        top = all_levels[0]
        for level in all_levels[1:]:
            top = jnp.maximum(top, level)
        upper = lower = 0.0
        for level, quotient in zip(all_levels, all_quotients):
            weight = jnp.exp2(level - top)
            upper = upper + weight * quotient
            lower = lower + weight
        out[:, columns] = jnp.where(live, upper / lower, 0.0).astype(bf16)


def combined(parts, suffix, request_row):
    slots = parts[0].shape[0]
    return pl.pallas_call(
        combine_kernel,
        out_shape=jax.ShapeDtypeStruct((slots, H * HD), bf16),
        in_specs=[VMEM] * (len(parts) + 3),
        out_specs=VMEM,
        compiler_params=PARAMS,
    )(*parts, *suffix, request_row)


def per_device(queries, suffix_keys, suffix_values, prefix_keys, prefix_values, slot_request):
    slots = queries.shape[0]
    request_row = slot_request.reshape(1, slots)
    own = jnp.concatenate([prefix_keys, prefix_values], axis=0)[None]

    far = [by_xor(own, dz=4), by_ring(own, dz=2), by_ring(own, dz=-2)]
    others = [
        by_xor(queries, dx=1, dz=1),
        by_xor(queries, dx=1),
        by_xor(queries, dz=1),
    ]
    query, *suffix = own_part(queries, suffix_keys, suffix_values, request_row)
    first = jnp.concatenate([own, *far], axis=0)

    half_a, half_b = first[:2], first[2:]
    a_x = by_xor(half_a, dx=2)
    b_y = [by_ring(half_b, dy=1), by_ring(half_b, dy=-1), by_xor(half_b, dy=2)]
    first_c = by_xor(first, dc=1)
    pool, totals, peaks = first_fold(query, others, first)

    second_a = jnp.concatenate([half_a, a_x], axis=0)
    second_b = jnp.concatenate([half_b, *b_y], axis=0)
    a_y = [by_ring(second_a, dy=1), by_ring(second_a, dy=-1), by_xor(second_a, dy=2)]
    b_x = by_xor(second_b, dx=2)
    second = [a_x, *b_y]
    second_c = by_xor(jnp.concatenate(second, axis=0), dc=1)
    totals = folded(pool, peaks, totals, [first_c, *second])

    third_c = by_xor(jnp.concatenate(a_y[:2], axis=0), dc=1)
    totals = folded(pool, peaks, totals, [second_c, *a_y[:2]])
    last = [a_y[2], b_x]
    last_c = by_xor(jnp.concatenate(last, axis=0), dc=1)
    totals = folded(pool, peaks, totals, [third_c, *last])

    every = [first, first_c, *second, second_c, *a_y[:2], third_c, *last, last_c]
    parts = []
    for j in (1, 2, 3, 0):
        parts.append(last_fold(pool[j], peaks[j], totals[j], [last_c], every))
    parts = [
        parts[3],
        by_xor(parts[0], dx=1, dz=1),
        by_xor(parts[1], dx=1),
        by_xor(parts[2], dz=1),
    ]
    return combined(parts, suffix, request_row)


def solution(mesh):
    placed = (
        P(AXES, None),
        P(AXES, None),
        P(AXES, None),
        P(AXES, None),
        P(AXES, None),
        P(AXES),
    )
    return jax.shard_map(
        per_device, mesh=mesh, in_specs=placed, out_specs=P(AXES, None), check_vma=False
    )
```

time: 133 us -> 205 us (1.54)
  the two profiles are of different devices: /device:TPU:32 before, /device:TPU:27 now
where the time goes in v2:
time: 205 us; the launch traced here: 203 us
  Pallas kernels  156 us (76%)
  starting transfers between devices  31.7 us (15%)
  waiting for transfers between devices  12.9 us (6%)
    pallas_call x4, Pallas kernels, last_fold(): pl.pallas_call(lambda *refs: last_kernel(len(pieces), len(every), *refs),...  134 us
    ppermute x21, starting transfers between devices, moved(): return lax.ppermute(array, AXES, sorted(pairs))  31.7 us
    pallas_call x3, Pallas kernels, folded(): pl.pallas_call(lambda *refs: fold_kernel(len(pieces), *refs), out_shape=(...  18.3 us
    ppermute x21, waiting for transfers between devices, moved(): return lax.ppermute(array, AXES, sorted(pairs))  12.9 us
  transfers between devices with their start and end apart: 21, of which 4 were waited for; matrix products, arithmetic and copies ran while one was open for 0% of the time, Pallas kernels for 60%

profile of v2, /device:TPU:27, one launch (start us, length us, event | category | flops | bytes accessed | tf_op | source)
XLA Modules:
  0.0 202.7 jit_solution(14865628625826218282)
XLA Ops:
  0.0 0.8 maximum_bitcast_fusion
  0.8 6.9 %collective-permute-start.3 = (bf16[1,256,128]{2,1,0:T(8,128)(2,1)S(1)}, bf16[1,256,128]{2,1,0:T(8,128)(2,1)S(1)}, u32[]{:S(2)}, u32[]{:S(2)}) collective-permute-start(bf16[1,256,128]{2,1,0:T(8,128)(2,1)S(1)} %maximum_bitcast_fusion), channel_id=1, source_target_pairs={{0,8},{1,9},{2,10},{3,11},{4,12},{5,13},{6,14},{7,15},{8,0},{9,1},... | collective-permute-start | bytes 196616 | tf_op jit(solution)/shard_map/ppermute | solution.py:33
  7.7 1.2 collective-permute-start.4
  8.9 2.4 %collective-permute-start.5 = (bf16[1,256,128]{2,1,0:T(8,128)(2,1)S(1)}, bf16[1,256,128]{2,1,0:T(8,128)(2,1)S(1)}, u32[]{:S(2)}, u32[]{:S(2)}) collective-permute-start(bf16[1,256,128]{2,1,0:T(8,128)(2,1)S(1)} %maximum_bitcast_fusion), channel_id=1, source_target_pairs={{0,12},{1,13},{2,14},{3,15},{4,0},{5,1},{6,2},{7,3},{8,4},{9,5},{1... | collective-permute-start | bytes 196616 | tf_op jit(solution)/shard_map/ppermute | solution.py:33
  11.3 0.7 collective-permute-start
  12.0 1.2 collective-permute-start.1
  13.2 0.7 collective-permute-start.2
  14.0 1.9 collective-permute-start.6
  16.1 0.6 copy-done.2
  16.7 0.5 shard_map.64
  17.2 6.5 %collective-permute-done.6.refs_9_.refs_6_ = bf16[2,256,128]{2,1,0:T(8,128)(2,1)S(1)} collective-permute-done((bf16[2,256,128]{2,1,0:T(8,128)(2,1)S(1)}, bf16[2,256,128]{2,1,0:T(8,128)(2,1)S(1)}, u32[]{:S(2)}, u32[]{:S(2)}) %collective-permute-start.6) | collective-permute-done | bytes 131104 | tf_op jit(solution)/shard_map/ppermute | solution.py:33
  23.6 0.5 collective-permute-start.12
  24.2 0.7 collective-permute-start.13
  24.9 4.3 %collective-permute-done.12.refs_11_.refs_8_ = bf16[2,256,128]{2,1,0:T(8,128)(2,1)S(1)} collective-permute-done((bf16[2,256,128]{2,1,0:T(8,128)(2,1)S(1)}, bf16[2,256,128]{2,1,0:T(8,128)(2,1)S(1)}, u32[]{:S(2)}, u32[]{:S(2)}) %collective-permute-start.12) | collective-permute-done | bytes 131104 | tf_op jit(solution)/shard_map/ppermute | solution.py:33
  29.3 1.5 collective-permute-done.13.refs_12_.refs_9_
  30.8 2.2 %collective-permute-start.10 = (bf16[4,256,128]{2,1,0:T(8,128)(2,1)S(1)}, bf16[4,256,128]{2,1,0:T(8,128)(2,1)S(1)}, u32[]{:S(2)}, u32[]{:S(2)}) collective-permute-start(bf16[4,256,128]{2,1,0:T(8,128)(2,1)S(1)} %get-tuple-element.57), channel_id=1, source_target_pairs={{0,64},{1,65},{2,66},{3,67},{4,68},{5,69},{6,70},{7,71},{8,72},{9,... | collective-permute-start | bytes 786440 | tf_op jit(solution)/shard_map/ppermute | solution.py:33
  33.1 3.6 %collective-permute-start.16 = (bf16[4,256,128]{2,1,0:T(8,128)(2,1)S(1)}, bf16[4,256,128]{2,1,0:T(8,128)(2,1)S(1)}, u32[]{:S(2)}, u32[]{:S(2)}) collective-permute-start(bf16[4,256,128]{2,1,0:T(8,128)(2,1)S(1)} %get-tuple-element.58.refs_4_), channel_id=1, source_target_pairs={{0,1},{1,0},{2,3},{3,2},{4,5},{5,4},{6,7},{7,6},{8,9},{9,8},{10,11... | collective-permute-start | bytes 786440 | tf_op jit(solution)/shard_map/ppermute | solution.py:33
  36.7 1.1 collective-permute-start.14
  37.8 1.6 shard_map.65
  39.5 1.9 collective-permute-start.15
  41.5 5.0 %collective-permute-start.9 = (bf16[8,256,128]{2,1,0:T(8,128)(2,1)S(1)}, bf16[8,256,128]{2,1,0:T(8,128)(2,1)S(1)}, u32[]{:S(2)}, u32[]{:S(2)}) collective-permute-start(bf16[8,256,128]{2,1,0:T(8,128)(2,1)S(1)} %pad_maximum_fusion.1), channel_id=1, source_target_pairs={{0,1},{1,0},{2,3},{3,2},{4,5},{5,4},{6,7},{7,6},{8,9},{9,8},{10,11... | collective-permute-start | bytes 1572872 | tf_op jit(solution)/shard_map/ppermute | solution.py:33
  46.5 4.6 %shard_map.66 = (f32[512,256]{1,0:T(8,128)S(1)}, f32[512,256]{1,0:T(8,128)S(1)}, f32[512,256]{1,0:T(8,128)S(1)}, f32[512,256]{1,0:T(8,128)S(1)}) custom-call(bf16[512,256]{1,0:T(8,128)(2,1)S(1)} %get-tuple-element.31.refs_0_, ...), custom_call_target="tpu_custom_call", output_to_operand_aliasing={{0}: (13, {}), {1}: (14, {}), {2}: (15, {}), {3}: (16, {})} | custom-call | flops 3221225472 | bytes 4194304 | tf_op jit(solution)/shard_map/pallas_call | solution.py:194
  51.1 0.6 collective-permute-done.14.refs_10_.refs_15_
  51.8 1.0 collective-permute-start.17
  52.7 6.1 %shard_map.67 = (f32[512,256]{1,0:T(8,128)S(1)}, f32[512,256]{1,0:T(8,128)S(1)}, f32[512,256]{1,0:T(8,128)S(1)}, f32[512,256]{1,0:T(8,128)S(1)}) custom-call(bf16[512,256]{1,0:T(8,128)(2,1)S(1)} %get-tuple-element.31.refs_0_, ...), custom_call_target="tpu_custom_call", output_to_operand_aliasing={{0}: (11, {}), {1}: (12, {}), {2}: (13, {}), {3}: (14, {})} | custom-call | flops 4294967296 | bytes 4194304 | tf_op jit(solution)/shard_map/pallas_call | solution.py:194
  58.8 7.6 %shard_map.68 = (f32[512,256]{1,0:T(8,128)S(1)}, f32[512,256]{1,0:T(8,128)S(1)}, f32[512,256]{1,0:T(8,128)S(1)}, f32[512,256]{1,0:T(8,128)S(1)}) custom-call(bf16[512,256]{1,0:T(8,128)(2,1)S(1)} %get-tuple-element.31.refs_0_, ...), custom_call_target="tpu_custom_call", output_to_operand_aliasing={{0}: (11, {}), {1}: (12, {}), {2}: (13, {}), {3}: (14, {})} | custom-call | flops 5368709120 | bytes 4194304 | tf_op jit(solution)/shard_map/pallas_call | solution.py:194
  66.4 33.6 %shard_map.72 = bf16[64,1152]{1,0:T(8,128)(2,1)S(1)} custom-call(bf16[512,256]{1,0:T(8,128)(2,1)S(1)} %get-tuple-element.35.refs_3_.refs_0_, f32[512,128]{1,0:T(8,128)S(1)} %get-tuple-element.38.refs_7_.refs_1_, f32[512,256]{1,0:T(8,128)S(1)} %get-tuple-element.54.refs_2_, bf16[12,256,128]{2,1,0:T(8,128)(2,1)S(1)} %collective-permute-done.17.refs_3_.refs_16_, ...), custom_call_target="tpu_custom_call" | custom-call | flops 805306368 | bytes 1048576 | tf_op jit(solution)/shard_map/pallas_call | solution.py:269
  100.2 33.6 %shard_map.71 = bf16[64,1152]{1,0:T(8,128)(2,1)S(1)} custom-call(bf16[512,256]{1,0:T(8,128)(2,1)S(1)} %get-tuple-element.34.refs_2_.refs_0_, f32[512,128]{1,0:T(8,128)S(1)} %get-tuple-element.37.refs_6_.refs_1_, f32[512,256]{1,0:T(8,128)S(1)} %get-tuple-element.53.refs_2_, bf16[12,256,128]{2,1,0:T(8,128)(2,1)S(1)} %collective-permute-done.17.refs_3_.refs_16_, ...), custom_call_target="tpu_custom_call" | custom-call | flops 805306368 | bytes 1048576 | tf_op jit(solution)/shard_map/pallas_call | solution.py:269
  133.8 0.3 collective-permute-start.19
  134.1 33.6 %shard_map.70 = bf16[64,1152]{1,0:T(8,128)(2,1)S(1)} custom-call(bf16[512,256]{1,0:T(8,128)(2,1)S(1)} %get-tuple-element.33.refs_1_.refs_0_, f32[512,128]{1,0:T(8,128)S(1)} %get-tuple-element.36.refs_5_.refs_1_, f32[512,256]{1,0:T(8,128)S(1)} %get-tuple-element.52.refs_2_, bf16[12,256,128]{2,1,0:T(8,128)(2,1)S(1)} %collective-permute-done.17.refs_3_.refs_16_, ...), custom_call_target="tpu_custom_call" | custom-call | flops 805306368 | bytes 1048576 | tf_op jit(solution)/shard_map/pallas_call | solution.py:269
  167.8 33.6 %shard_map.69.refs_0_ = bf16[64,1152]{1,0:T(8,128)(2,1)S(1)} custom-call(bf16[512,256]{1,0:T(8,128)(2,1)S(1)} %get-tuple-element.31.refs_0_, f32[512,128]{1,0:T(8,128)S(1)} %get-tuple-element.32.refs_4_.refs_1_, f32[512,256]{1,0:T(8,128)S(1)} %get-tuple-element.51.refs_2_, bf16[12,256,128]{2,1,0:T(8,128)(2,1)S(1)} %collective-permute-done.17.refs_3_.refs_16_, ...), custom_call_target="tpu_custom_call" | custom-call | flops 805306368 | bytes 1048576 | tf_op jit(solution)/shard_map/pallas_call | solution.py:269
  201.4 1.2 shard_map.73
  (39 shorter events, 0.7 us)
Async XLA Ops:
  0.0 11.3 %copy-start.1 = (bf16[64,1024]{1,0:T(8,128)(2,1)S(1)}, bf16[64,1024]{1,0:T(8,128)(2,1)}, u32[]{:S(2)}) copy-start(bf16[64,1024]{1,0:T(8,128)(2,1)} %queries.1) | copy-start | bytes 393220
  0.8 12.4 %collective-permute-start.3 = (bf16[1,256,128]{2,1,0:T(8,128)(2,1)S(1)}, bf16[1,256,128]{2,1,0:T(8,128)(2,1)S(1)}, u32[]{:S(2)}, u32[]{:S(2)}) collective-permute-start(bf16[1,256,128]{2,1,0:T(8,128)(2,1)S(1)} %maximum_bitcast_fusion), channel_id=1, source_target_pairs={{0,8},{1,9},{2,10},{3,11},{4,12},{5,13},{6,14},{7,15},{8,0},{9,1},... | collective-permute-start | bytes 196616 | tf_op jit(solution)/shard_map/ppermute | solution.py:33
  7.7 6.3 %collective-permute-start.4 = (bf16[1,256,128]{2,1,0:T(8,128)(2,1)S(1)}, bf16[1,256,128]{2,1,0:T(8,128)(2,1)S(1)}, u32[]{:S(2)}, u32[]{:S(2)}) collective-permute-start(bf16[1,256,128]{2,1,0:T(8,128)(2,1)S(1)} %maximum_bitcast_fusion), channel_id=1, source_target_pairs={{0,4},{1,5},{2,6},{3,7},{4,8},{5,9},{6,10},{7,11},{8,12},{9,13},{1... | collective-permute-start | bytes 196616 | tf_op jit(solution)/shard_map/ppermute | solution.py:33
  8.9 7.0 %collective-permute-start.5 = (bf16[1,256,128]{2,1,0:T(8,128)(2,1)S(1)}, bf16[1,256,128]{2,1,0:T(8,128)(2,1)S(1)}, u32[]{:S(2)}, u32[]{:S(2)}) collective-permute-start(bf16[1,256,128]{2,1,0:T(8,128)(2,1)S(1)} %maximum_bitcast_fusion), channel_id=1, source_target_pairs={{0,12},{1,13},{2,14},{3,15},{4,0},{5,1},{6,2},{7,3},{8,4},{9,5},{1... | collective-permute-start | bytes 196616 | tf_op jit(solution)/shard_map/ppermute | solution.py:33
  11.3 19.5 %collective-permute-start = (bf16[64,1024]{1,0:T(8,128)(2,1)S(1)}, bf16[64,1024]{1,0:T(8,128)(2,1)S(1)}, u32[]{:S(2)}, u32[]{:S(2)}) collective-permute-start(bf16[64,1024]{1,0:T(8,128)(2,1)S(1)} %copy-done.1), channel_id=1, source_target_pairs={{0,130},{1,131},{2,128},{3,129},{4,134},{5,135},{6,132},{7,133},{8... | collective-permute-start | bytes 393224 | tf_op jit(solution)/shard_map/ppermute | solution.py:33
  12.0 21.1 %collective-permute-start.1 = (bf16[64,1024]{1,0:T(8,128)(2,1)S(1)}, bf16[64,1024]{1,0:T(8,128)(2,1)S(1)}, u32[]{:S(2)}, u32[]{:S(2)}) collective-permute-start(bf16[64,1024]{1,0:T(8,128)(2,1)S(1)} %copy-done.1), channel_id=1, source_target_pairs={{0,128},{1,129},{2,130},{3,131},{4,132},{5,133},{6,134},{7,135},{8... | collective-permute-start | bytes 393224 | tf_op jit(solution)/shard_map/ppermute | solution.py:33
  13.2 23.5 %collective-permute-start.2 = (bf16[64,1024]{1,0:T(8,128)(2,1)S(1)}, bf16[64,1024]{1,0:T(8,128)(2,1)S(1)}, u32[]{:S(2)}, u32[]{:S(2)}) collective-permute-start(bf16[64,1024]{1,0:T(8,128)(2,1)S(1)} %copy-done.1), channel_id=1, source_target_pairs={{0,2},{1,3},{2,0},{3,1},{4,6},{5,7},{6,4},{7,5},{8,10},{9,11},{10,... | collective-permute-start | bytes 393224 | tf_op jit(solution)/shard_map/ppermute | solution.py:33
  14.0 9.7 %collective-permute-start.6 = (bf16[2,256,128]{2,1,0:T(8,128)(2,1)S(1)}, bf16[2,256,128]{2,1,0:T(8,128)(2,1)S(1)}, u32[]{:S(2)}, u32[]{:S(2)}) collective-permute-start(bf16[2,256,128]{2,1,0:T(8,128)(2,1)S(1)} %pad_maximum_fusion.6), channel_id=1, source_target_pairs={{0,16},{1,17},{2,18},{3,19},{4,20},{5,21},{6,22},{7,23},{8,24},{9,... | collective-permute-start | bytes 393224 | tf_op jit(solution)/shard_map/ppermute | solution.py:33
  15.9 0.7 copy-start.2
  16.0 0.7 copy-start.3
  16.0 0.7 copy-start
  16.0 8.1 %collective-permute-start.11 = (bf16[2,256,128]{2,1,0:T(8,128)(2,1)S(1)}, bf16[2,256,128]{2,1,0:T(8,128)(2,1)S(1)}, u32[]{:S(2)}, u32[]{:S(2)}) collective-permute-start(bf16[2,256,128]{2,1,0:T(8,128)(2,1)S(1)} %get-tuple-element.59), channel_id=1, source_target_pairs={{0,32},{1,33},{2,34},{3,35},{4,36},{5,37},{6,38},{7,39},{8,40},{9,... | collective-permute-start | bytes 393224 | tf_op jit(solution)/shard_map/ppermute | solution.py:33
  23.6 5.6 %collective-permute-start.12 = (bf16[2,256,128]{2,1,0:T(8,128)(2,1)S(1)}, bf16[2,256,128]{2,1,0:T(8,128)(2,1)S(1)}, u32[]{:S(2)}, u32[]{:S(2)}) collective-permute-start(bf16[2,256,128]{2,1,0:T(8,128)(2,1)S(1)} %get-tuple-element.59), channel_id=1, source_target_pairs={{0,96},{1,97},{2,98},{3,99},{4,100},{5,101},{6,102},{7,103},{8,104... | collective-permute-start | bytes 393224 | tf_op jit(solution)/shard_map/ppermute | solution.py:33
  24.2 6.6 %collective-permute-start.13 = (bf16[2,256,128]{2,1,0:T(8,128)(2,1)S(1)}, bf16[2,256,128]{2,1,0:T(8,128)(2,1)S(1)}, u32[]{:S(2)}, u32[]{:S(2)}) collective-permute-start(bf16[2,256,128]{2,1,0:T(8,128)(2,1)S(1)} %get-tuple-element.59), channel_id=1, source_target_pairs={{0,64},{1,65},{2,66},{3,67},{4,68},{5,69},{6,70},{7,71},{8,72},{9,... | collective-permute-start | bytes 393224 | tf_op jit(solution)/shard_map/ppermute | solution.py:33
  29.2 10.3 %collective-permute-start.7 = (bf16[4,256,128]{2,1,0:T(8,128)(2,1)S(1)}, bf16[4,256,128]{2,1,0:T(8,128)(2,1)S(1)}, u32[]{:S(2)}, u32[]{:S(2)}) collective-permute-start(bf16[4,256,128]{2,1,0:T(8,128)(2,1)S(1)} %get-tuple-element.57), channel_id=1, source_target_pairs={{0,32},{1,33},{2,34},{3,35},{4,36},{5,37},{6,38},{7,39},{8,40},{9,... | collective-permute-start | bytes 786440 | tf_op jit(solution)/shard_map/ppermute | solution.py:33
  30.8 10.7 %collective-permute-start.8 = (bf16[4,256,128]{2,1,0:T(8,128)(2,1)S(1)}, bf16[4,256,128]{2,1,0:T(8,128)(2,1)S(1)}, u32[]{:S(2)}, u32[]{:S(2)}) collective-permute-start(bf16[4,256,128]{2,1,0:T(8,128)(2,1)S(1)} %get-tuple-element.57), channel_id=1, source_target_pairs={{0,96},{1,97},{2,98},{3,99},{4,100},{5,101},{6,102},{7,103},{8,104... | collective-permute-start | bytes 786440 | tf_op jit(solution)/shard_map/ppermute | solution.py:33
  30.8 20.3 %collective-permute-start.10 = (bf16[4,256,128]{2,1,0:T(8,128)(2,1)S(1)}, bf16[4,256,128]{2,1,0:T(8,128)(2,1)S(1)}, u32[]{:S(2)}, u32[]{:S(2)}) collective-permute-start(bf16[4,256,128]{2,1,0:T(8,128)(2,1)S(1)} %get-tuple-element.57), channel_id=1, source_target_pairs={{0,64},{1,65},{2,66},{3,67},{4,68},{5,69},{6,70},{7,71},{8,72},{9,... | collective-permute-start | bytes 786440 | tf_op jit(solution)/shard_map/ppermute | solution.py:33
  33.1 13.4 %collective-permute-start.16 = (bf16[4,256,128]{2,1,0:T(8,128)(2,1)S(1)}, bf16[4,256,128]{2,1,0:T(8,128)(2,1)S(1)}, u32[]{:S(2)}, u32[]{:S(2)}) collective-permute-start(bf16[4,256,128]{2,1,0:T(8,128)(2,1)S(1)} %get-tuple-element.58.refs_4_), channel_id=1, source_target_pairs={{0,1},{1,0},{2,3},{3,2},{4,5},{5,4},{6,7},{7,6},{8,9},{9,8},{10,11... | collective-permute-start | bytes 786440 | tf_op jit(solution)/shard_map/ppermute | solution.py:33
  36.7 15.0 %collective-permute-start.14 = (bf16[8,256,128]{2,1,0:T(8,128)(2,1)S(1)}, bf16[8,256,128]{2,1,0:T(8,128)(2,1)S(1)}, u32[]{:S(2)}, u32[]{:S(2)}) collective-permute-start(bf16[8,256,128]{2,1,0:T(8,128)(2,1)S(1)} %constant_dynamic-update-slice_fusion.2), channel_id=1, source_target_pairs={{0,16},{1,17},{2,18},{3,19},{4,20},{5,21},{6,22},{7,23},{8,24},{9,... | collective-permute-start | bytes 1572872 | tf_op jit(solution)/shard_map/ppermute | solution.py:33
  39.5 13.2 %collective-permute-start.15 = (bf16[8,256,128]{2,1,0:T(8,128)(2,1)S(1)}, bf16[8,256,128]{2,1,0:T(8,128)(2,1)S(1)}, u32[]{:S(2)}, u32[]{:S(2)}) collective-permute-start(bf16[8,256,128]{2,1,0:T(8,128)(2,1)S(1)} %pad_maximum_fusion.2), channel_id=1, source_target_pairs={{0,1},{1,0},{2,3},{3,2},{4,5},{5,4},{6,7},{7,6},{8,9},{9,8},{10,11... | collective-permute-start | bytes 1572872 | tf_op jit(solution)/shard_map/ppermute | solution.py:33
  41.5 17.3 %collective-permute-start.9 = (bf16[8,256,128]{2,1,0:T(8,128)(2,1)S(1)}, bf16[8,256,128]{2,1,0:T(8,128)(2,1)S(1)}, u32[]{:S(2)}, u32[]{:S(2)}) collective-permute-start(bf16[8,256,128]{2,1,0:T(8,128)(2,1)S(1)} %pad_maximum_fusion.1), channel_id=1, source_target_pairs={{0,1},{1,0},{2,3},{3,2},{4,5},{5,4},{6,7},{7,6},{8,9},{9,8},{10,11... | collective-permute-start | bytes 1572872 | tf_op jit(solution)/shard_map/ppermute | solution.py:33
  51.8 14.7 %collective-permute-start.17 = (bf16[12,256,128]{2,1,0:T(8,128)(2,1)S(1)}, bf16[12,256,128]{2,1,0:T(8,128)(2,1)S(1)}, u32[]{:S(2)}, u32[]{:S(2)}) collective-permute-start(bf16[12,256,128]{2,1,0:T(8,128)(2,1)S(1)} %pad_maximum_fusion), channel_id=1, source_target_pairs={{0,1},{1,0},{2,3},{3,2},{4,5},{5,4},{6,7},{7,6},{8,9},{9,8},{10,11... | collective-permute-start | bytes 2359304 | tf_op jit(solution)/shard_map/ppermute | solution.py:33
  100.1 101.3 %collective-permute-start.20 = (bf16[64,1152]{1,0:T(8,128)(2,1)S(1)}, bf16[64,1152]{1,0:T(8,128)(2,1)S(1)}, u32[]{:S(2)}, u32[]{:S(2)}) collective-permute-start(bf16[64,1152]{1,0:T(8,128)(2,1)S(1)} %shard_map.72), channel_id=1, source_target_pairs={{0,2},{1,3},{2,0},{3,1},{4,6},{5,7},{6,4},{7,5},{8,10},{9,11},{10,... | collective-permute-start | bytes 442376 | tf_op jit(solution)/shard_map/ppermute | solution.py:33
  133.8 67.6 %collective-permute-start.19 = (bf16[64,1152]{1,0:T(8,128)(2,1)S(1)}, bf16[64,1152]{1,0:T(8,128)(2,1)S(1)}, u32[]{:S(2)}, u32[]{:S(2)}) collective-permute-start(bf16[64,1152]{1,0:T(8,128)(2,1)S(1)} %shard_map.71), channel_id=1, source_target_pairs={{0,128},{1,129},{2,130},{3,131},{4,132},{5,133},{6,134},{7,135},{8... | collective-permute-start | bytes 442376 | tf_op jit(solution)/shard_map/ppermute | solution.py:33
  167.7 33.7 %collective-permute-start.18 = (bf16[64,1152]{1,0:T(8,128)(2,1)S(1)}, bf16[64,1152]{1,0:T(8,128)(2,1)S(1)}, u32[]{:S(2)}, u32[]{:S(2)}) collective-permute-start(bf16[64,1152]{1,0:T(8,128)(2,1)S(1)} %shard_map.70), channel_id=1, source_target_pairs={{0,130},{1,131},{2,128},{3,129},{4,134},{5,135},{6,132},{7,133},{8... | collective-permute-start | bytes 442376 | tf_op jit(solution)/shard_map/ppermute | solution.py:33

commit v3 on v2

--- a/solution.py
+++ b/solution.py
@@ -81,7 +81,14 @@
     )
 
 
-def own_kernel(queries, suffix_keys, suffix_values, request, query, quotient, level):
+def own_kernel(*refs):
+    sources, (query, quotient, level), held, semaphores = refs[:4], refs[4:7], refs[7:11], refs[11]
+    copies = [pltpu.make_async_copy(a, b, semaphores.at[i]) for i, (a, b) in enumerate(zip(sources, held))]
+    for copy in copies:
+        copy.start()
+    for copy in copies:
+        copy.wait()
+    queries, suffix_keys, suffix_values, request = held
     slots = queries.shape[0]
     prepare(queries, query)
     own, across, row, column = request_column(request[...], slots)
@@ -104,8 +111,12 @@
     return pl.pallas_call(
         own_kernel,
         out_shape=(jax.ShapeDtypeStruct((H * slots, 2 * HD), bf16), shape, shape),
-        in_specs=[VMEM] * 4,
+        in_specs=[pl.BlockSpec(memory_space=pl.ANY)] * 4,
         out_specs=(VMEM,) * 3,
+        scratch_shapes=[
+            pltpu.VMEM(a.shape, a.dtype) for a in (queries, suffix_keys, suffix_values, request_row)
+        ]
+        + [pltpu.SemaphoreType.DMA((4,))],
         compiler_params=PARAMS,
         cost_estimate=cost(H * slots, 512),
     )(queries, suffix_keys, suffix_values, request_row)
@@ -160,11 +171,12 @@
         compiler_params=PARAMS,
         cost_estimate=cost(POOL * rows, key_count + 512),
     )(query, *others, piece)
-    return [query, *outs[: POOL - 1]], outs[POOL - 1 : 2 * POOL - 1], outs[2 * POOL - 1 :]
-
-
-def add_tile(query, total, peak, keys, values, rows, span):
-    weights = jnp.exp2(scored(query[rows, :], keys[span, :]) - wide(peak[rows, :], KEY_TILE))
+    return [query, *outs[: POOL - 1]], list(outs[POOL - 1 : 2 * POOL - 1]), outs[2 * POOL - 1 :]
+
+
+def add_tile(query, total, peak, keys, values, rows, start, length=KEY_TILE):
+    span = pl.ds(start, length)
+    weights = jnp.exp2(scored(query[rows, :], keys[span, :]) - wide(peak[rows, :], length))
     total[rows, :] += jnp.dot(weights.astype(bf16), values[span, :], preferred_element_type=f32)
 
 
@@ -176,20 +188,24 @@
         total[...] = held[...]
     key_count = load_pieces(pieces, keys, values)
 
-    def step(i, _):
-        span = pl.ds(pl.multiple_of(i * KEY_TILE, KEY_TILE), KEY_TILE)
+    def add_all(key_start, length):
         for j in range(POOL):
             for start in range(0, queries[j].shape[0], ROW_TILE):
-                add_tile(queries[j], totals[j], peaks[j], keys, values, pl.ds(start, ROW_TILE), span)
+                rows = pl.ds(start, ROW_TILE)
+                add_tile(queries[j], totals[j], peaks[j], keys, values, rows, key_start, length)
+
+    def step(i, _):
+        add_all(pl.multiple_of(i * KEY_TILE, KEY_TILE), KEY_TILE)
         return 0
 
     lax.fori_loop(0, key_count // KEY_TILE, step, 0)
+    if key_count % KEY_TILE:
+        add_all(key_count - key_count % KEY_TILE, key_count % KEY_TILE)
 
 
 def folded(queries, peaks, totals, pieces):
     rows = queries[0].shape[0]
     key_count = sum(p.shape[0] for p in pieces) * BLOCK
-    assert key_count % KEY_TILE == 0
     at = 2 * POOL + len(pieces)
     return pl.pallas_call(
         lambda *refs: fold_kernel(len(pieces), *refs),
@@ -240,7 +256,8 @@
     peak[...] = peak_in[...]
     for key_start in range(0, key_count, KEY_TILE):
         for start in range(0, query.shape[0], ROW_TILE):
-            add_tile(query, total, peak, keys, values, pl.ds(start, ROW_TILE), pl.ds(key_start, KEY_TILE))
+            length = min(KEY_TILE, key_count - key_start)
+            add_tile(query, total, peak, keys, values, pl.ds(start, ROW_TILE), key_start, length)
 
     @pl.when(jnp.logical_not(jnp.max(total[:, HD:]) < MASS_LIMIT))
     def _():
@@ -334,33 +351,33 @@
         by_xor(queries, dx=1),
         by_xor(queries, dz=1),
     ]
-    query, *suffix = own_part(queries, suffix_keys, suffix_values, request_row)
     first = jnp.concatenate([own, *far], axis=0)
+    first, held_queries = lax.optimization_barrier((first, queries))
+    query, *suffix = own_part(held_queries, suffix_keys, suffix_values, request_row)
 
     half_a, half_b = first[:2], first[2:]
-    a_x = by_xor(half_a, dx=2)
+    by_x = by_xor(first, dx=2)
     b_y = [by_ring(half_b, dy=1), by_ring(half_b, dy=-1), by_xor(half_b, dy=2)]
-    first_c = by_xor(first, dc=1)
+    by_x, *b_y = lax.optimization_barrier((by_x, *b_y))
+    all_b_y = jnp.concatenate(b_y, axis=0)
+    b_x = by_xor(all_b_y, dx=2)
+    both_a = jnp.concatenate([half_a, by_x[:2]], axis=0)
+    a_y = [by_ring(both_a, dy=1), by_ring(both_a, dy=-1), by_xor(both_a, dy=2)]
     pool, totals, peaks = first_fold(query, others, first)
 
-    second_a = jnp.concatenate([half_a, a_x], axis=0)
-    second_b = jnp.concatenate([half_b, *b_y], axis=0)
-    a_y = [by_ring(second_a, dy=1), by_ring(second_a, dy=-1), by_xor(second_a, dy=2)]
-    b_x = by_xor(second_b, dx=2)
-    second = [a_x, *b_y]
-    second_c = by_xor(jnp.concatenate(second, axis=0), dc=1)
-    totals = folded(pool, peaks, totals, [first_c, *second])
-
-    third_c = by_xor(jnp.concatenate(a_y[:2], axis=0), dc=1)
-    totals = folded(pool, peaks, totals, [second_c, *a_y[:2]])
-    last = [a_y[2], b_x]
-    last_c = by_xor(jnp.concatenate(last, axis=0), dc=1)
-    totals = folded(pool, peaks, totals, [third_c, *last])
-
-    every = [first, first_c, *second, second_c, *a_y[:2], third_c, *last, last_c]
+    early = jnp.concatenate([first, by_x, all_b_y], axis=0)
+    early, totals[0] = lax.optimization_barrier((early, totals[0]))
+    early_c = by_xor(early, dc=1)
+    totals = list(folded(pool, peaks, totals, [by_x, all_b_y]))
+    totals = list(folded(pool, peaks, totals, [early_c]))
+    *late, totals[0] = lax.optimization_barrier((*a_y, b_x, totals[0]))
+    late_c = by_xor(jnp.concatenate(late, axis=0), dc=1)
+    totals = list(folded(pool, peaks, totals, late))
+
+    every = [first, by_x, all_b_y, early_c, *late, late_c]
     parts = []
     for j in (1, 2, 3, 0):
-        parts.append(last_fold(pool[j], peaks[j], totals[j], [last_c], every))
+        parts.append(last_fold(pool[j], peaks[j], totals[j], [late_c], every))
     parts = [
         parts[3],
         by_xor(parts[0], dx=1, dz=1),

time: 205 us -> 192 us (0.937)
  the two profiles are of different devices: /device:TPU:27 before, /device:TPU:45 now
where the time goes in v3:
time: 192 us; the launch traced here: 190 us
  Pallas kernels  156 us (81%)
  starting transfers between devices  25.7 us (13%)
  waiting for transfers between devices  6.55 us (3%)
    pallas_call x4, Pallas kernels, last_fold(): pl.pallas_call(lambda *refs: last_kernel(len(pieces), len(every), *refs),...  136 us
    ppermute x19, starting transfers between devices, moved(): return lax.ppermute(array, AXES, sorted(pairs))  25.7 us
    pallas_call x3, Pallas kernels, folded(): pl.pallas_call(lambda *refs: fold_kernel(len(pieces), *refs), out_shape=(...  16.9 us
    ppermute x19, waiting for transfers between devices, moved(): return lax.ppermute(array, AXES, sorted(pairs))  6.55 us
  transfers between devices with their start and end apart: 19, of which 4 were waited for; matrix products, arithmetic and copies ran while one was open for 0% of the time, Pallas kernels for 64%

profile of v3, /device:TPU:45, one launch (start us, length us, event | category | flops | bytes accessed | tf_op | source)
XLA Modules:
  0.0 190.2 jit_solution(9952260013667961146)
XLA Ops:
  0.0 0.8 maximum_bitcast_fusion
  0.8 5.1 %collective-permute-start.2 = (bf16[1,256,128]{2,1,0:T(8,128)(2,1)S(1)}, bf16[1,256,128]{2,1,0:T(8,128)(2,1)S(1)}, u32[]{:S(2)}, u32[]{:S(2)}) collective-permute-start(bf16[1,256,128]{2,1,0:T(8,128)(2,1)S(1)} %maximum_bitcast_fusion), channel_id=1, source_target_pairs={{0,12},{1,13},{2,14},{3,15},{4,0},{5,1},{6,2},{7,3},{8,4},{9,5},{1... | collective-permute-start | bytes 196616 | tf_op jit(solution)/shard_map/ppermute | solution.py:33
  6.0 3.3 %collective-permute-start = (bf16[1,256,128]{2,1,0:T(8,128)(2,1)S(1)}, bf16[1,256,128]{2,1,0:T(8,128)(2,1)S(1)}, u32[]{:S(2)}, u32[]{:S(2)}) collective-permute-start(bf16[1,256,128]{2,1,0:T(8,128)(2,1)S(1)} %maximum_bitcast_fusion), channel_id=1, source_target_pairs={{0,8},{1,9},{2,10},{3,11},{4,12},{5,13},{6,14},{7,15},{8,0},{9,1},... | collective-permute-start | bytes 196616 | tf_op jit(solution)/shard_map/ppermute | solution.py:33
  9.2 1.4 collective-permute-start.3
  10.6 0.7 collective-permute-start.5
  11.3 0.5 collective-permute-start.4
  11.9 1.2 collective-permute-done
  13.1 0.3 collective-permute-start.6
  13.4 2.1 %collective-permute-start.9 = (bf16[2,256,128]{2,1,0:T(8,128)(2,1)S(1)}, bf16[2,256,128]{2,1,0:T(8,128)(2,1)S(1)}, u32[]{:S(2)}, u32[]{:S(2)}) collective-permute-start(bf16[2,256,128]{2,1,0:T(8,128)(2,1)S(1)} %get-tuple-element.84), channel_id=1, source_target_pairs={{0,64},{1,65},{2,66},{3,67},{4,68},{5,69},{6,70},{7,71},{8,72},{9,... | collective-permute-start | bytes 393224 | tf_op jit(solution)/shard_map/ppermute | solution.py:33
  15.5 0.7 shard_map.64
  16.3 1.2 collective-permute-done.3.refs_1_
  17.5 0.2 collective-permute-start.8
  17.7 2.4 %collective-permute-done.5.refs_3_ = bf16[64,1024]{1,0:T(8,128)(2,1)S(1)} collective-permute-done((bf16[64,1024]{1,0:T(8,128)(2,1)}, bf16[64,1024]{1,0:T(8,128)(2,1)S(1)}, u32[]{:S(2)}, u32[]{:S(2)}) %collective-permute-start.5) | collective-permute-done | bytes 131104 | tf_op jit(solution)/shard_map/ppermute | solution.py:33
  20.0 1.3 collective-permute-start.7
  21.3 1.6 shard_map.65
  22.9 1.8 collective-permute-done.7
  24.9 1.9 %collective-permute-start.14 = (bf16[14,256,128]{2,1,0:T(8,128)(2,1)S(1)}, bf16[14,256,128]{2,1,0:T(8,128)(2,1)S(1)}, u32[]{:S(2)}, u32[]{:S(2)}) collective-permute-start(bf16[14,256,128]{2,1,0:T(8,128)(2,1)S(1)} %get-tuple-element.59), channel_id=1, source_target_pairs={{0,1},{1,0},{2,3},{3,2},{4,5},{5,4},{6,7},{7,6},{8,9},{9,8},{10,11... | collective-permute-start | bytes 2752520 | tf_op jit(solution)/shard_map/ppermute | solution.py:33
  26.9 1.6 collective-permute-start.12
  28.6 1.4 collective-permute-start.11
  30.0 0.7 collective-permute-start.10
  30.7 2.3 %collective-permute-start.13 = (bf16[6,256,128]{2,1,0:T(8,128)(2,1)S(1)}, bf16[6,256,128]{2,1,0:T(8,128)(2,1)S(1)}, u32[]{:S(2)}, u32[]{:S(2)}) collective-permute-start(bf16[6,256,128]{2,1,0:T(8,128)(2,1)S(1)} %get-tuple-element.86.refs_9_.refs_6_), channel_id=1, source_target_pairs={{0,16},{1,17},{2,18},{3,19},{4,20},{5,21},{6,22},{7,23},{8,24},{9,... | collective-permute-start | bytes 1179656 | tf_op jit(solution)/shard_map/ppermute | solution.py:33
  32.9 4.2 %shard_map.66 = (f32[512,256]{1,0:T(8,128)S(1)}, f32[512,256]{1,0:T(8,128)S(1)}, f32[512,256]{1,0:T(8,128)S(1)}, f32[512,256]{1,0:T(8,128)S(1)}) custom-call(bf16[512,256]{1,0:T(8,128)(2,1)S(1)} %get-tuple-element.45.refs_0_, ...), custom_call_target="tpu_custom_call", output_to_operand_aliasing={{0}: (10, {}), {1}: (11, {}), {2}: (12, {}), {3}: (13, {})} | custom-call | flops 2684354560 | bytes 4194304 | tf_op jit(solution)/shard_map/pallas_call | solution.py:210
  37.1 5.6 %shard_map.67 = (f32[512,256]{1,0:T(8,128)S(1)}, f32[512,256]{1,0:T(8,128)S(1)}, f32[512,256]{1,0:T(8,128)S(1)}, f32[512,256]{1,0:T(8,128)S(1)}) custom-call(bf16[512,256]{1,0:T(8,128)(2,1)S(1)} %get-tuple-element.45.refs_0_, ...), custom_call_target="tpu_custom_call", output_to_operand_aliasing={{0}: (9, {}), {1}: (10, {}), {2}: (11, {}), {3}: (12, {})} | custom-call | flops 3758096384 | bytes 4194304 | tf_op jit(solution)/shard_map/pallas_call | solution.py:210
  42.9 1.0 collective-permute-start.15
  43.9 7.1 %shard_map.68 = (f32[512,256]{1,0:T(8,128)S(1)}, f32[512,256]{1,0:T(8,128)S(1)}, f32[512,256]{1,0:T(8,128)S(1)}, f32[512,256]{1,0:T(8,128)S(1)}) custom-call(bf16[512,256]{1,0:T(8,128)(2,1)S(1)} %get-tuple-element.45.refs_0_, ...), custom_call_target="tpu_custom_call", output_to_operand_aliasing={{0}: (12, {}), {1}: (13, {}), {2}: (14, {}), {3}: (15, {})} | custom-call | flops 4831838208 | bytes 4194304 | tf_op jit(solution)/shard_map/pallas_call | solution.py:210
  51.1 34.0 %shard_map.70 = bf16[64,1152]{1,0:T(8,128)(2,1)S(1)} custom-call(bf16[512,256]{1,0:T(8,128)(2,1)S(1)} %get-tuple-element.48.refs_1_.refs_0_, f32[512,128]{1,0:T(8,128)S(1)} %get-tuple-element.51.refs_5_.refs_1_, f32[512,256]{1,0:T(8,128)S(1)} %get-tuple-element.78.refs_2_, bf16[18,256,128]{2,1,0:T(8,128)(2,1)S(1)} %collective-permute-done.15.refs_3_.refs_12_, ...), custom_call_target="tpu_custom_call" | custom-call | flops 1207959552 | bytes 1048576 | tf_op jit(solution)/shard_map/pallas_call | solution.py:286
  85.1 0.3 collective-permute-start.16
  85.4 34.0 %shard_map.71 = bf16[64,1152]{1,0:T(8,128)(2,1)S(1)} custom-call(bf16[512,256]{1,0:T(8,128)(2,1)S(1)} %get-tuple-element.49.refs_2_.refs_0_, f32[512,128]{1,0:T(8,128)S(1)} %get-tuple-element.52.refs_6_.refs_1_, f32[512,256]{1,0:T(8,128)S(1)} %get-tuple-element.79.refs_2_, bf16[18,256,128]{2,1,0:T(8,128)(2,1)S(1)} %collective-permute-done.15.refs_3_.refs_12_, ...), custom_call_target="tpu_custom_call" | custom-call | flops 1207959552 | bytes 1048576 | tf_op jit(solution)/shard_map/pallas_call | solution.py:286
  119.4 1.4 collective-permute-start.17
  120.8 34.0 %shard_map.72 = bf16[64,1152]{1,0:T(8,128)(2,1)S(1)} custom-call(bf16[512,256]{1,0:T(8,128)(2,1)S(1)} %get-tuple-element.50.refs_3_.refs_0_, f32[512,128]{1,0:T(8,128)S(1)} %get-tuple-element.53.refs_7_.refs_1_, f32[512,256]{1,0:T(8,128)S(1)} %get-tuple-element.80.refs_2_, bf16[18,256,128]{2,1,0:T(8,128)(2,1)S(1)} %collective-permute-done.15.refs_3_.refs_12_, ...), custom_call_target="tpu_custom_call" | custom-call | flops 1207959552 | bytes 1048576 | tf_op jit(solution)/shard_map/pallas_call | solution.py:286
  154.9 34.0 %shard_map.69.refs_0_ = bf16[64,1152]{1,0:T(8,128)(2,1)S(1)} custom-call(bf16[512,256]{1,0:T(8,128)(2,1)S(1)} %get-tuple-element.45.refs_0_, f32[512,128]{1,0:T(8,128)S(1)} %get-tuple-element.47.refs_4_.refs_1_, f32[512,256]{1,0:T(8,128)S(1)} %get-tuple-element.77.refs_2_, bf16[18,256,128]{2,1,0:T(8,128)(2,1)S(1)} %collective-permute-done.15.refs_3_.refs_12_, ...), custom_call_target="tpu_custom_call" | custom-call | flops 1207959552 | bytes 1048576 | tf_op jit(solution)/shard_map/pallas_call | solution.py:286
  189.0 1.2 shard_map.73
  (35 shorter events, 0.6 us)
Async XLA Ops:
  0.0 15.5 %copy-start.1 = (bf16[64,1024]{1,0:T(8,128)(2,1)S(1)}, bf16[64,1024]{1,0:T(8,128)(2,1)}, u32[]{:S(2)}) copy-start(bf16[64,1024]{1,0:T(8,128)(2,1)} %refs_0_) | copy-start | bytes 393220
  0.0 15.5 %copy-start = (s32[64]{0:T(128)S(1)}, s32[64]{0:T(128)}, u32[]{:S(2)}) copy-start(s32[64]{0:T(128)} %param.11) | copy-start | bytes 772
  0.0 15.5 %copy-start.3 = (bf16[64,128]{1,0:T(8,128)(2,1)S(1)}, bf16[64,128]{1,0:T(8,128)(2,1)}, u32[]{:S(2)}) copy-start(bf16[64,128]{1,0:T(8,128)(2,1)} %refs_2_.1) | copy-start | bytes 49156
  0.0 15.5 %copy-start.2 = (bf16[64,128]{1,0:T(8,128)(2,1)S(1)}, bf16[64,128]{1,0:T(8,128)(2,1)}, u32[]{:S(2)}) copy-start(bf16[64,128]{1,0:T(8,128)(2,1)} %refs_1_.1) | copy-start | bytes 49156
  0.8 10.5 %collective-permute-start.2 = (bf16[1,256,128]{2,1,0:T(8,128)(2,1)S(1)}, bf16[1,256,128]{2,1,0:T(8,128)(2,1)S(1)}, u32[]{:S(2)}, u32[]{:S(2)}) collective-permute-start(bf16[1,256,128]{2,1,0:T(8,128)(2,1)S(1)} %maximum_bitcast_fusion), channel_id=1, source_target_pairs={{0,12},{1,13},{2,14},{3,15},{4,0},{5,1},{6,2},{7,3},{8,4},{9,5},{1... | collective-permute-start | bytes 196616 | tf_op jit(solution)/shard_map/ppermute | solution.py:33
  6.0 5.9 %collective-permute-start.1 = (bf16[1,256,128]{2,1,0:T(8,128)(2,1)S(1)}, bf16[1,256,128]{2,1,0:T(8,128)(2,1)S(1)}, u32[]{:S(2)}, u32[]{:S(2)}) collective-permute-start(bf16[1,256,128]{2,1,0:T(8,128)(2,1)S(1)} %maximum_bitcast_fusion), channel_id=1, source_target_pairs={{0,4},{1,5},{2,6},{3,7},{4,8},{5,9},{6,10},{7,11},{8,12},{9,13},{1... | collective-permute-start | bytes 196616 | tf_op jit(solution)/shard_map/ppermute | solution.py:33
  6.0 7.1 %collective-permute-start = (bf16[1,256,128]{2,1,0:T(8,128)(2,1)S(1)}, bf16[1,256,128]{2,1,0:T(8,128)(2,1)S(1)}, u32[]{:S(2)}, u32[]{:S(2)}) collective-permute-start(bf16[1,256,128]{2,1,0:T(8,128)(2,1)S(1)} %maximum_bitcast_fusion), channel_id=1, source_target_pairs={{0,8},{1,9},{2,10},{3,11},{4,12},{5,13},{6,14},{7,15},{8,0},{9,1},... | collective-permute-start | bytes 196616 | tf_op jit(solution)/shard_map/ppermute | solution.py:33
  9.2 8.3 %collective-permute-start.3 = (bf16[64,1024]{1,0:T(8,128)(2,1)}, bf16[64,1024]{1,0:T(8,128)(2,1)S(1)}, u32[]{:S(2)}, u32[]{:S(2)}) collective-permute-start(bf16[64,1024]{1,0:T(8,128)(2,1)} %refs_0_), channel_id=1, source_target_pairs={{0,130},{1,131},{2,128},{3,129},{4,134},{5,135},{6,132},{7,133},{8... | collective-permute-start | bytes 393224 | tf_op jit(solution)/shard_map/ppermute | solution.py:33
  10.6 9.5 %collective-permute-start.5 = (bf16[64,1024]{1,0:T(8,128)(2,1)}, bf16[64,1024]{1,0:T(8,128)(2,1)S(1)}, u32[]{:S(2)}, u32[]{:S(2)}) collective-permute-start(bf16[64,1024]{1,0:T(8,128)(2,1)} %refs_0_), channel_id=1, source_target_pairs={{0,2},{1,3},{2,0},{3,1},{4,6},{5,7},{6,4},{7,5},{8,10},{9,11},{10,... | collective-permute-start | bytes 393224 | tf_op jit(solution)/shard_map/ppermute | solution.py:33
  11.3 10.0 %collective-permute-start.4 = (bf16[64,1024]{1,0:T(8,128)(2,1)}, bf16[64,1024]{1,0:T(8,128)(2,1)S(1)}, u32[]{:S(2)}, u32[]{:S(2)}) collective-permute-start(bf16[64,1024]{1,0:T(8,128)(2,1)} %refs_0_), channel_id=1, source_target_pairs={{0,128},{1,129},{2,130},{3,131},{4,132},{5,133},{6,134},{7,135},{8... | collective-permute-start | bytes 393224 | tf_op jit(solution)/shard_map/ppermute | solution.py:33
  13.1 11.6 %collective-permute-start.6 = (bf16[4,256,128]{2,1,0:T(8,128)(2,1)S(1)}, bf16[4,256,128]{2,1,0:T(8,128)(2,1)S(1)}, u32[]{:S(2)}, u32[]{:S(2)}) collective-permute-start(bf16[4,256,128]{2,1,0:T(8,128)(2,1)S(1)} %pad_maximum_fusion.1.refs_4_), channel_id=1, source_target_pairs={{0,16},{1,17},{2,18},{3,19},{4,20},{5,21},{6,22},{7,23},{8,24},{9,... | collective-permute-start | bytes 786440 | tf_op jit(solution)/shard_map/ppermute | solution.py:33
  13.4 9.5 %collective-permute-start.9 = (bf16[2,256,128]{2,1,0:T(8,128)(2,1)S(1)}, bf16[2,256,128]{2,1,0:T(8,128)(2,1)S(1)}, u32[]{:S(2)}, u32[]{:S(2)}) collective-permute-start(bf16[2,256,128]{2,1,0:T(8,128)(2,1)S(1)} %get-tuple-element.84), channel_id=1, source_target_pairs={{0,64},{1,65},{2,66},{3,67},{4,68},{5,69},{6,70},{7,71},{8,72},{9,... | collective-permute-start | bytes 393224 | tf_op jit(solution)/shard_map/ppermute | solution.py:33
  17.5 5.4 %collective-permute-start.8 = (bf16[2,256,128]{2,1,0:T(8,128)(2,1)S(1)}, bf16[2,256,128]{2,1,0:T(8,128)(2,1)S(1)}, u32[]{:S(2)}, u32[]{:S(2)}) collective-permute-start(bf16[2,256,128]{2,1,0:T(8,128)(2,1)S(1)} %get-tuple-element.84), channel_id=1, source_target_pairs={{0,96},{1,97},{2,98},{3,99},{4,100},{5,101},{6,102},{7,103},{8,104... | collective-permute-start | bytes 393224 | tf_op jit(solution)/shard_map/ppermute | solution.py:33
  20.0 4.7 %collective-permute-start.7 = (bf16[2,256,128]{2,1,0:T(8,128)(2,1)S(1)}, bf16[2,256,128]{2,1,0:T(8,128)(2,1)S(1)}, u32[]{:S(2)}, u32[]{:S(2)}) collective-permute-start(bf16[2,256,128]{2,1,0:T(8,128)(2,1)S(1)} %get-tuple-element.84), channel_id=1, source_target_pairs={{0,32},{1,33},{2,34},{3,35},{4,36},{5,37},{6,38},{7,39},{8,40},{9,... | collective-permute-start | bytes 393224 | tf_op jit(solution)/shard_map/ppermute | solution.py:33
  24.9 12.2 %collective-permute-start.14 = (bf16[14,256,128]{2,1,0:T(8,128)(2,1)S(1)}, bf16[14,256,128]{2,1,0:T(8,128)(2,1)S(1)}, u32[]{:S(2)}, u32[]{:S(2)}) collective-permute-start(bf16[14,256,128]{2,1,0:T(8,128)(2,1)S(1)} %get-tuple-element.59), channel_id=1, source_target_pairs={{0,1},{1,0},{2,3},{3,2},{4,5},{5,4},{6,7},{7,6},{8,9},{9,8},{10,11... | collective-permute-start | bytes 2752520 | tf_op jit(solution)/shard_map/ppermute | solution.py:33
  26.9 15.8 %collective-permute-start.12 = (bf16[4,256,128]{2,1,0:T(8,128)(2,1)S(1)}, bf16[4,256,128]{2,1,0:T(8,128)(2,1)S(1)}, u32[]{:S(2)}, u32[]{:S(2)}) collective-permute-start(bf16[4,256,128]{2,1,0:T(8,128)(2,1)S(1)} %pad_maximum_fusion.2), channel_id=1, source_target_pairs={{0,64},{1,65},{2,66},{3,67},{4,68},{5,69},{6,70},{7,71},{8,72},{9,... | collective-permute-start | bytes 786440 | tf_op jit(solution)/shard_map/ppermute | solution.py:33
  28.6 14.2 %collective-permute-start.11 = (bf16[4,256,128]{2,1,0:T(8,128)(2,1)S(1)}, bf16[4,256,128]{2,1,0:T(8,128)(2,1)S(1)}, u32[]{:S(2)}, u32[]{:S(2)}) collective-permute-start(bf16[4,256,128]{2,1,0:T(8,128)(2,1)S(1)} %pad_maximum_fusion.2), channel_id=1, source_target_pairs={{0,96},{1,97},{2,98},{3,99},{4,100},{5,101},{6,102},{7,103},{8,104... | collective-permute-start | bytes 786440 | tf_op jit(solution)/shard_map/ppermute | solution.py:33
  30.0 12.8 %collective-permute-start.10 = (bf16[4,256,128]{2,1,0:T(8,128)(2,1)S(1)}, bf16[4,256,128]{2,1,0:T(8,128)(2,1)S(1)}, u32[]{:S(2)}, u32[]{:S(2)}) collective-permute-start(bf16[4,256,128]{2,1,0:T(8,128)(2,1)S(1)} %pad_maximum_fusion.2), channel_id=1, source_target_pairs={{0,32},{1,33},{2,34},{3,35},{4,36},{5,37},{6,38},{7,39},{8,40},{9,... | collective-permute-start | bytes 786440 | tf_op jit(solution)/shard_map/ppermute | solution.py:33
  30.7 12.1 %collective-permute-start.13 = (bf16[6,256,128]{2,1,0:T(8,128)(2,1)S(1)}, bf16[6,256,128]{2,1,0:T(8,128)(2,1)S(1)}, u32[]{:S(2)}, u32[]{:S(2)}) collective-permute-start(bf16[6,256,128]{2,1,0:T(8,128)(2,1)S(1)} %get-tuple-element.86.refs_9_.refs_6_), channel_id=1, source_target_pairs={{0,16},{1,17},{2,18},{3,19},{4,20},{5,21},{6,22},{7,23},{8,24},{9,... | collective-permute-start | bytes 1179656 | tf_op jit(solution)/shard_map/ppermute | solution.py:33
  42.9 8.1 %collective-permute-start.15 = (bf16[18,256,128]{2,1,0:T(8,128)(2,1)S(1)}, bf16[18,256,128]{2,1,0:T(8,128)(2,1)S(1)}, u32[]{:S(2)}, u32[]{:S(2)}) collective-permute-start(bf16[18,256,128]{2,1,0:T(8,128)(2,1)S(1)} %pad_maximum_fusion), channel_id=1, source_target_pairs={{0,1},{1,0},{2,3},{3,2},{4,5},{5,4},{6,7},{7,6},{8,9},{9,8},{10,11... | collective-permute-start | bytes 3538952 | tf_op jit(solution)/shard_map/ppermute | solution.py:33
  85.1 103.9 %collective-permute-start.16 = (bf16[64,1152]{1,0:T(8,128)(2,1)S(1)}, bf16[64,1152]{1,0:T(8,128)(2,1)S(1)}, u32[]{:S(2)}, u32[]{:S(2)}) collective-permute-start(bf16[64,1152]{1,0:T(8,128)(2,1)S(1)} %shard_map.70), channel_id=1, source_target_pairs={{0,130},{1,131},{2,128},{3,129},{4,134},{5,135},{6,132},{7,133},{8... | collective-permute-start | bytes 442376 | tf_op jit(solution)/shard_map/ppermute | solution.py:33
  119.4 69.6 %collective-permute-start.17 = (bf16[64,1152]{1,0:T(8,128)(2,1)S(1)}, bf16[64,1152]{1,0:T(8,128)(2,1)S(1)}, u32[]{:S(2)}, u32[]{:S(2)}) collective-permute-start(bf16[64,1152]{1,0:T(8,128)(2,1)S(1)} %shard_map.71), channel_id=1, source_target_pairs={{0,128},{1,129},{2,130},{3,131},{4,132},{5,133},{6,134},{7,135},{8... | collective-permute-start | bytes 442376 | tf_op jit(solution)/shard_map/ppermute | solution.py:33
  154.8 34.1 %collective-permute-start.18 = (bf16[64,1152]{1,0:T(8,128)(2,1)S(1)}, bf16[64,1152]{1,0:T(8,128)(2,1)S(1)}, u32[]{:S(2)}, u32[]{:S(2)}) collective-permute-start(bf16[64,1152]{1,0:T(8,128)(2,1)S(1)} %shard_map.72), channel_id=1, source_target_pairs={{0,2},{1,3},{2,0},{3,1},{4,6},{5,7},{6,4},{7,5},{8,10},{9,11},{10,... | collective-permute-start | bytes 442376 | tf_op jit(solution)/shard_map/ppermute | solution.py:33
